TPU v7x, 128 devices: a whole 4x4x4 slice. The times are simulated.
128 devices in a mesh: heads: 4 (over x), ctx: 32 (over y, z, core).
Axes of the slice: x: 4, y: 4, z: 4, core: 2. Of those that a mesh axis runs over, the one named last changes fastest.
Arguments:
- queries: bfloat16 [32, 128, 192], P('ctx', 'heads')
- latent_store_cache: bfloat16 [8, 49152, 576], P(None, 'ctx')
- new_latent: bfloat16 [32, 576], replicated
- cache_lengths: int32 [8], replicated, may hold values from 1 to 49152, 196608 in all
- key_up: bfloat16 [128, 128, 512], P('heads'), may hold values from -0.5 to 0.5
- value_up: bfloat16 [128, 512, 128], P('heads'), may hold values from -0.25 to 0.25
- out_proj: bfloat16 [16384, 7168], P('heads', 'ctx'), may hold values from -0.046875 to 0.046875
Outputs:
- attention_result: bfloat16 [32, 7168], P(None, 'ctx')
Inputs may be any that keep to these rules, and one draw needn't show every extreme that they name: Request b has cache_lengths[b] valid positions at the start of its cache; some request has exactly 49152.
All inputs are finite; a program needn't handle non-finite values.
Results may differ from a plain program's by a relative error of at most 0.023.
Values may be sent and summed in bfloat16 or wider, within the bound.
A program may use at most 320 MiB of HBM per device.

v0:
```python
import math

import jax
import jax.numpy as jnp
from jax import lax
from jax.sharding import PartitionSpec as P

NEG = -1e30


def combined_all(value, axis, join):
    gathered = jax.tree.map(
        lambda a, kind: lax.all_gather(a.astype(kind), axis),
        value,
        (jnp.bfloat16, jnp.bfloat16, jnp.bfloat16),
    )

    def take(source):
        return jax.tree.map(
            lambda a, own: lax.dynamic_index_in_dim(a, source, 0, False).astype(own.dtype),
            gathered,
            value,
        )

    return lax.fori_loop(
        1, lax.axis_size(axis), lambda source, state: join(state, take(source)), take(0)
    )


def absorb(rows_in, key_up):
    nope = key_up.shape[1]
    q_lat = jnp.einsum(
        "rhd,hdc->rhc", rows_in[:, :, :nope], key_up, preferred_element_type=jnp.float32
    )
    return jnp.concatenate([q_lat.astype(jnp.bfloat16), rows_in[:, :, nope:]], axis=2)


def attend(whole, latent_store_cache, new_latent, cache_lengths, latent, scale):
    reqs, ctx_dev, width = latent_store_cache.shape
    rows, heads_here = (whole.shape[0], whole.shape[1])
    steps = rows // reqs
    request_query = whole.reshape(reqs, steps * heads_here, width)
    fresh = new_latent.reshape(reqs, steps, width)
    here = lax.axis_index("ctx")
    scores = (
        jnp.einsum(
            "str,sdr->std", request_query, latent_store_cache, preferred_element_type=jnp.float32
        )
        * scale
    )
    position = here * ctx_dev + jnp.arange(ctx_dev, dtype=jnp.int32)
    valid = position[None, None, :] < cache_lengths[:, None, None]
    near = (
        jnp.einsum("bqc,bjc->bqj", request_query, fresh, preferred_element_type=jnp.float32) * scale
    )
    step_of = jnp.arange(steps * heads_here, dtype=jnp.int32) // heads_here
    valid_near = ((jnp.arange(steps, dtype=jnp.int32)[None, :] <= step_of[:, None]) & (here == 0))[
        None, :, :
    ]
    masked = jnp.where(valid, scores, NEG)
    masked_nearby = jnp.where(valid_near, near, NEG)
    top = jnp.maximum(jnp.max(masked, axis=2), jnp.max(masked_nearby, axis=2))
    weight = jnp.where(valid, jnp.exp(masked - top[:, :, None]), 0.0)
    weight_near = jnp.where(valid_near, jnp.exp(masked_nearby - top[:, :, None]), 0.0)
    total = jnp.sum(weight, axis=2) + jnp.sum(weight_near, axis=2)
    summed = jnp.einsum(
        "ilv,ivz->ilz",
        weight.astype(jnp.bfloat16),
        latent_store_cache[:, :, :latent],
        preferred_element_type=jnp.float32,
    )
    summed = summed + jnp.einsum(
        "bqj,bjc->bqc",
        weight_near.astype(jnp.bfloat16),
        fresh[:, :, :latent],
        preferred_element_type=jnp.float32,
    )
    return (
        top.reshape(rows, heads_here),
        total.reshape(rows, heads_here),
        summed.reshape(rows, heads_here, latent),
    )


def combine_states(first, second):
    top_a, total_a, summed_a = first
    top_b, total_b, summed_b = second
    top = jnp.maximum(top_a, top_b)
    factor_a = jnp.exp(top_a - top)
    factor_b = jnp.exp(top_b - top)
    total = total_a * factor_a + total_b * factor_b
    summed = summed_a * factor_a[:, :, None] + summed_b * factor_b[:, :, None]
    return (top, total, summed)


def project_values(latent_rows, value_up):
    return jnp.einsum(
        "rhc,hcv->rhv", latent_rows, value_up.astype(jnp.float32), precision=lax.Precision.HIGHEST
    )


def local(queries, latent_store_cache, new_latent, cache_lengths, key_up, value_up, out_proj):
    latent = key_up.shape[2]
    scale = 1.0 / math.sqrt(queries.shape[2])
    whole = lax.all_gather(absorb(queries, key_up), "ctx", axis=0, tiled=True)
    top, total, summed = attend(whole, latent_store_cache, new_latent, cache_lengths, latent, scale)
    rows = summed.shape[0]
    top, total, summed = combined_all((top, total, summed), "ctx", combine_states)
    o_lat = summed / total[:, :, None]
    head_out = project_values(o_lat, value_up).astype(jnp.bfloat16).reshape(rows, -1)
    partial_out = jnp.dot(head_out, out_proj, preferred_element_type=jnp.float32)
    return lax.psum(partial_out, "heads").astype(jnp.bfloat16)


def solution(mesh):
    in_specs = (
        P("ctx", "heads", None),
        P(None, "ctx", None),
        P(),
        P(),
        P("heads", None, None),
        P("heads", None, None),
        P("heads", "ctx"),
    )
    out_specs = P(None, "ctx")
    return jax.shard_map(local, mesh=mesh, in_specs=in_specs, out_specs=out_specs, check_vma=False)
```

profile of v0, /device:TPU:1, one launch (start us, length us, event | category | flops | bytes accessed | tf_op | source)
XLA Modules:
  0.0 341.2 jit_solution(8766951887130770035)
XLA Ops:
  11.1 46.7 %all-gather.3.cloned.1.call-done = bf16[32,32,576]{2,1,0:T(8,128)(2,1)} async-done(((bf16[1,32,576]{2,1,0:T(8,128)(2,1)}), bf16[32,32,576]{2,1,0:T(8,128)(2,1)}) %all-gather.3.cloned.1.call-update) | async-done | bytes 1179664 | tf_op jit(solution)/shard_map/all_gather | solution.py:105
  59.7 11.0 %fusion.5 = (f32[8,128]{1,0:T(8,128)S(1)}, f32[8,128,1536]{2,1,0:T(8,128)}) fusion(pred[8,1536]{1,0:T(8,128)(4,1)S(1)} %broadcast_compare_fusion, bf16[8,128,576]{2,1,0:T(8,128)(2,1)} %bitcast.58, bf16[8,1536,576]{1,2,0:T(8,128)(2,1)} %param.10), kind=kOutput, calls=%fused_computation.12 | convolution fusion | flops 1816656896 | bytes 21643264 | tf_op jit(solution)/shard_map/str,sdr->std/dot_general | solution.py:46
  70.7 12.0 %fusion.3 = f32[8,128,512]{2,1,0:T(8,128)} fusion(bf16[8,1536,576]{1,2,0:T(8,128)(2,1)} %param.10, f32[8,128,1536]{2,1,0:T(8,128)} %get-tuple-element.205, f32[8,128]{1,0:T(8,128)S(1)} %get-tuple-element.203, pred[8,1536]{1,0:T(8,128)(4,1)S(1)} %broadcast_compare_fusion), kind=kOutput, calls=%fused_computation.8 | convolution fusion | flops 1618477056 | bytes 20987904 | tf_op jit(solution)/shard_map/ilv,ivz->ilz/dot_general | solution.py:66
  85.9 4.5 %fusion.7 = f32[8,128]{1,0:T(8,128)S(1)} fusion(f32[8,128,1536]{2,1,0:T(8,128)} %get-tuple-element.205, f32[8,128]{1,0:T(8,128)S(1)} %get-tuple-element.203, pred[8,1536]{1,0:T(8,128)(4,1)S(1)} %broadcast_compare_fusion), kind=kLoop, calls=%fused_computation.14 | loop fusion | flops 7863296 | bytes 6311936 | tf_op jit(solution)/shard_map/reduce_sum | solution.py:65
  90.6 24.2 %all_gather.16 = bf16[32,32,32]{2,1,0:T(8,128)(2,1)S(1)} all-gather(bf16[1,32,32]{2,1,0:T(8,128)(2,1)S(1)} %convert_element_type.121), channel_id=1, replica_groups=mesh['heads'=4,'ctx'=32] {'ctx'}, dimensions={0}, use_global_device_ids=true | all-gather | bytes 67584 | tf_op jit(solution)/shard_map/all_gather | solution.py:13
  114.8 22.8 %all_gather.17 = bf16[32,32,32]{2,1,0:T(8,128)(2,1)S(1)} all-gather(bf16[1,32,32]{2,1,0:T(8,128)(2,1)S(1)} %convert_element_type.125), channel_id=1, replica_groups=mesh['heads'=4,'ctx'=32] {'ctx'}, dimensions={0}, use_global_device_ids=true | all-gather | bytes 67584 | tf_op jit(solution)/shard_map/all_gather | solution.py:13
  137.5 62.6 %all-gather.5.cloned.1.call-done = bf16[32,32,32,512]{3,2,1,0:T(8,128)(2,1)} async-done(((bf16[1,32,32,512]{3,2,1,0:T(8,128)(2,1)}), bf16[32,32,32,512]{3,2,1,0:T(8,128)(2,1)}) %all-gather.5.cloned.1.call-update) | async-done | bytes 33554448 | tf_op jit(solution)/shard_map/all_gather | solution.py:13
  203.0 111.0 %while.19 = (s32[]{:T(128)}, f32[32,32]{1,0:T(8,128)S(1)}, f32[32,32]{1,0:T(8,128)S(1)}, f32[32,32,512]{2,1,0:T(8,128)}, bf16[32,32,32]{2,1,0:T(8,128)(2,1)S(1)}...) while((s32[]{:T(128)}, f32[32,32]{1,0:T(8,128)S(1)}, ...), condition=%wide.region_5.6_spmd, body=%wide.region_4.5_spmd.sunk | while | flops 2105349 | bytes 5279887 | solution.py:25
  203.0 3.6 %fusion.57 = f32[32,32,512]{2,1,0:T(8,128)} fusion(f32[32,32,512]{2,1,0:T(8,128)} %get-tuple-element.272, f32[32,32]{1,0:T(8,128)S(1)} %get-tuple-element.257, bf16[32,32,32,512]{3,2,1,0:T(8,128)(2,1)} %get-tuple-element.285, s32[]{:T(128)S(6)} %select_n.70, f32[32,32]{1,0:T(8,128)S(1)} %get-tuple-element.258), kind=kLoop, calls=%fused_computation.1.clone.1 | loop fusion | flops 2097152 | bytes 5251076 | tf_op jit(solution)/shard_map/while/body/eval_jaxpr/add | solution.py:92
  206.6 3.6 %fusion.57 = f32[32,32,512]{2,1,0:T(8,128)} fusion(f32[32,32,512]{2,1,0:T(8,128)} %get-tuple-element.272, f32[32,32]{1,0:T(8,128)S(1)} %get-tuple-element.257, bf16[32,32,32,512]{3,2,1,0:T(8,128)(2,1)} %get-tuple-element.285, s32[]{:T(128)S(6)} %select_n.70, f32[32,32]{1,0:T(8,128)S(1)} %get-tuple-element.258), kind=kLoop, calls=%fused_computation.1.clone.1 | loop fusion | flops 2097152 | bytes 5251076 | tf_op jit(solution)/shard_map/while/body/eval_jaxpr/add | solution.py:92
  210.1 3.6 %fusion.57 = f32[32,32,512]{2,1,0:T(8,128)} fusion(f32[32,32,512]{2,1,0:T(8,128)} %get-tuple-element.272, f32[32,32]{1,0:T(8,128)S(1)} %get-tuple-element.257, bf16[32,32,32,512]{3,2,1,0:T(8,128)(2,1)} %get-tuple-element.285, s32[]{:T(128)S(6)} %select_n.70, f32[32,32]{1,0:T(8,128)S(1)} %get-tuple-element.258), kind=kLoop, calls=%fused_computation.1.clone.1 | loop fusion | flops 2097152 | bytes 5251076 | tf_op jit(solution)/shard_map/while/body/eval_jaxpr/add | solution.py:92
  213.7 3.6 %fusion.57 = f32[32,32,512]{2,1,0:T(8,128)} fusion(f32[32,32,512]{2,1,0:T(8,128)} %get-tuple-element.272, f32[32,32]{1,0:T(8,128)S(1)} %get-tuple-element.257, bf16[32,32,32,512]{3,2,1,0:T(8,128)(2,1)} %get-tuple-element.285, s32[]{:T(128)S(6)} %select_n.70, f32[32,32]{1,0:T(8,128)S(1)} %get-tuple-element.258), kind=kLoop, calls=%fused_computation.1.clone.1 | loop fusion | flops 2097152 | bytes 5251076 | tf_op jit(solution)/shard_map/while/body/eval_jaxpr/add | solution.py:92
  217.3 3.6 %fusion.57 = f32[32,32,512]{2,1,0:T(8,128)} fusion(f32[32,32,512]{2,1,0:T(8,128)} %get-tuple-element.272, f32[32,32]{1,0:T(8,128)S(1)} %get-tuple-element.257, bf16[32,32,32,512]{3,2,1,0:T(8,128)(2,1)} %get-tuple-element.285, s32[]{:T(128)S(6)} %select_n.70, f32[32,32]{1,0:T(8,128)S(1)} %get-tuple-element.258), kind=kLoop, calls=%fused_computation.1.clone.1 | loop fusion | flops 2097152 | bytes 5251076 | tf_op jit(solution)/shard_map/while/body/eval_jaxpr/add | solution.py:92
  220.9 3.6 %fusion.57 = f32[32,32,512]{2,1,0:T(8,128)} fusion(f32[32,32,512]{2,1,0:T(8,128)} %get-tuple-element.272, f32[32,32]{1,0:T(8,128)S(1)} %get-tuple-element.257, bf16[32,32,32,512]{3,2,1,0:T(8,128)(2,1)} %get-tuple-element.285, s32[]{:T(128)S(6)} %select_n.70, f32[32,32]{1,0:T(8,128)S(1)} %get-tuple-element.258), kind=kLoop, calls=%fused_computation.1.clone.1 | loop fusion | flops 2097152 | bytes 5251076 | tf_op jit(solution)/shard_map/while/body/eval_jaxpr/add | solution.py:92
  224.5 3.6 %fusion.57 = f32[32,32,512]{2,1,0:T(8,128)} fusion(f32[32,32,512]{2,1,0:T(8,128)} %get-tuple-element.272, f32[32,32]{1,0:T(8,128)S(1)} %get-tuple-element.257, bf16[32,32,32,512]{3,2,1,0:T(8,128)(2,1)} %get-tuple-element.285, s32[]{:T(128)S(6)} %select_n.70, f32[32,32]{1,0:T(8,128)S(1)} %get-tuple-element.258), kind=kLoop, calls=%fused_computation.1.clone.1 | loop fusion | flops 2097152 | bytes 5251076 | tf_op jit(solution)/shard_map/while/body/eval_jaxpr/add | solution.py:92
  228.0 3.6 %fusion.57 = f32[32,32,512]{2,1,0:T(8,128)} fusion(f32[32,32,512]{2,1,0:T(8,128)} %get-tuple-element.272, f32[32,32]{1,0:T(8,128)S(1)} %get-tuple-element.257, bf16[32,32,32,512]{3,2,1,0:T(8,128)(2,1)} %get-tuple-element.285, s32[]{:T(128)S(6)} %select_n.70, f32[32,32]{1,0:T(8,128)S(1)} %get-tuple-element.258), kind=kLoop, calls=%fused_computation.1.clone.1 | loop fusion | flops 2097152 | bytes 5251076 | tf_op jit(solution)/shard_map/while/body/eval_jaxpr/add | solution.py:92
  231.6 3.6 %fusion.57 = f32[32,32,512]{2,1,0:T(8,128)} fusion(f32[32,32,512]{2,1,0:T(8,128)} %get-tuple-element.272, f32[32,32]{1,0:T(8,128)S(1)} %get-tuple-element.257, bf16[32,32,32,512]{3,2,1,0:T(8,128)(2,1)} %get-tuple-element.285, s32[]{:T(128)S(6)} %select_n.70, f32[32,32]{1,0:T(8,128)S(1)} %get-tuple-element.258), kind=kLoop, calls=%fused_computation.1.clone.1 | loop fusion | flops 2097152 | bytes 5251076 | tf_op jit(solution)/shard_map/while/body/eval_jaxpr/add | solution.py:92
  235.2 3.6 %fusion.57 = f32[32,32,512]{2,1,0:T(8,128)} fusion(f32[32,32,512]{2,1,0:T(8,128)} %get-tuple-element.272, f32[32,32]{1,0:T(8,128)S(1)} %get-tuple-element.257, bf16[32,32,32,512]{3,2,1,0:T(8,128)(2,1)} %get-tuple-element.285, s32[]{:T(128)S(6)} %select_n.70, f32[32,32]{1,0:T(8,128)S(1)} %get-tuple-element.258), kind=kLoop, calls=%fused_computation.1.clone.1 | loop fusion | flops 2097152 | bytes 5251076 | tf_op jit(solution)/shard_map/while/body/eval_jaxpr/add | solution.py:92
  238.8 3.6 %fusion.57 = f32[32,32,512]{2,1,0:T(8,128)} fusion(f32[32,32,512]{2,1,0:T(8,128)} %get-tuple-element.272, f32[32,32]{1,0:T(8,128)S(1)} %get-tuple-element.257, bf16[32,32,32,512]{3,2,1,0:T(8,128)(2,1)} %get-tuple-element.285, s32[]{:T(128)S(6)} %select_n.70, f32[32,32]{1,0:T(8,128)S(1)} %get-tuple-element.258), kind=kLoop, calls=%fused_computation.1.clone.1 | loop fusion | flops 2097152 | bytes 5251076 | tf_op jit(solution)/shard_map/while/body/eval_jaxpr/add | solution.py:92
  242.4 3.6 %fusion.57 = f32[32,32,512]{2,1,0:T(8,128)} fusion(f32[32,32,512]{2,1,0:T(8,128)} %get-tuple-element.272, f32[32,32]{1,0:T(8,128)S(1)} %get-tuple-element.257, bf16[32,32,32,512]{3,2,1,0:T(8,128)(2,1)} %get-tuple-element.285, s32[]{:T(128)S(6)} %select_n.70, f32[32,32]{1,0:T(8,128)S(1)} %get-tuple-element.258), kind=kLoop, calls=%fused_computation.1.clone.1 | loop fusion | flops 2097152 | bytes 5251076 | tf_op jit(solution)/shard_map/while/body/eval_jaxpr/add | solution.py:92
  245.9 3.6 %fusion.57 = f32[32,32,512]{2,1,0:T(8,128)} fusion(f32[32,32,512]{2,1,0:T(8,128)} %get-tuple-element.272, f32[32,32]{1,0:T(8,128)S(1)} %get-tuple-element.257, bf16[32,32,32,512]{3,2,1,0:T(8,128)(2,1)} %get-tuple-element.285, s32[]{:T(128)S(6)} %select_n.70, f32[32,32]{1,0:T(8,128)S(1)} %get-tuple-element.258), kind=kLoop, calls=%fused_computation.1.clone.1 | loop fusion | flops 2097152 | bytes 5251076 | tf_op jit(solution)/shard_map/while/body/eval_jaxpr/add | solution.py:92
  249.5 3.6 %fusion.57 = f32[32,32,512]{2,1,0:T(8,128)} fusion(f32[32,32,512]{2,1,0:T(8,128)} %get-tuple-element.272, f32[32,32]{1,0:T(8,128)S(1)} %get-tuple-element.257, bf16[32,32,32,512]{3,2,1,0:T(8,128)(2,1)} %get-tuple-element.285, s32[]{:T(128)S(6)} %select_n.70, f32[32,32]{1,0:T(8,128)S(1)} %get-tuple-element.258), kind=kLoop, calls=%fused_computation.1.clone.1 | loop fusion | flops 2097152 | bytes 5251076 | tf_op jit(solution)/shard_map/while/body/eval_jaxpr/add | solution.py:92
  253.1 3.6 %fusion.57 = f32[32,32,512]{2,1,0:T(8,128)} fusion(f32[32,32,512]{2,1,0:T(8,128)} %get-tuple-element.272, f32[32,32]{1,0:T(8,128)S(1)} %get-tuple-element.257, bf16[32,32,32,512]{3,2,1,0:T(8,128)(2,1)} %get-tuple-element.285, s32[]{:T(128)S(6)} %select_n.70, f32[32,32]{1,0:T(8,128)S(1)} %get-tuple-element.258), kind=kLoop, calls=%fused_computation.1.clone.1 | loop fusion | flops 2097152 | bytes 5251076 | tf_op jit(solution)/shard_map/while/body/eval_jaxpr/add | solution.py:92
  320.5 13.8 %psum.7 = bf16[32,224]{1,0:T(8,128)(2,1)} all-reduce(f32[32,224]{1,0:T(8,128)S(1)} %fusion.24), channel_id=1, replica_groups=mesh['heads'=4,'ctx'=32] {'heads'}, use_global_device_ids=true, to_apply=%region_6.7 | all-reduce | flops 7168 | bytes 43008 | tf_op jit(solution)/shard_map/psum | solution.py:112
  (83 shorter events, 76.5 us)
Async XLA Ops:
  6.5 313.3 %copy-start = (bf16[4096,224]{0,1:T(8,128)(2,1)S(1)}, bf16[4096,224]{0,1:T(8,128)(2,1)}, u32[]{:S(2)}) copy-start(bf16[4096,224]{0,1:T(8,128)(2,1)} %param.15) | copy-start | bytes 5505028
  6.5 3.7 %slice-start = ((bf16[1,32,192]{2,1,0:T(8,128)(2,1)}), bf16[1,32,64]{2,1,0:T(8,128)(2,1)S(1)}, s32[]{:S(2)}) async-start(bf16[1,32,192]{2,1,0:T(8,128)(2,1)} %param.9), calls=%async_computation.2 | async-start | bytes 16384 | tf_op jit(solution)/shard_map/slice | solution.py:35
  6.5 4.4 %copy-start.2 = (bf16[32,576]{1,0:T(8,128)(2,1)S(1)}, bf16[32,576]{1,0:T(8,128)(2,1)}, u32[]{:S(2)}) copy-start(bf16[32,576]{1,0:T(8,128)(2,1)} %param.11) | copy-start | bytes 110596
  6.5 4.5 %copy-start.3 = (s32[8]{0:T(128)S(1)}, s32[8]{0:T(128)}, u32[]{:S(2)}) copy-start(s32[8]{0:T(128)} %param.12) | copy-start | bytes 100
  6.5 51.3 %all-gather.3.cloned.1.call-start = ((), (), s32[]{:S(2)}) async-start(), calls=%async_computation | async-start | bytes 1351680 | tf_op jit(solution)/shard_map/all_gather | solution.py:105
  10.9 189.2 %all-gather.5.cloned.1.call-start = ((), (), s32[]{:S(2)}) async-start(), calls=%async_computation.1 | async-start | bytes 34603008 | tf_op jit(solution)/shard_map/all_gather | solution.py:13
  313.9 2.8 copy-start.1
Sparse Core Ops, SparseCore 0:
  11.0 46.7 all-gather.2
  86.0 114.1 all-gather.4
where the time goes:
time: 344 us; the launch traced here: 341 us
  other arithmetic  121 us (35%)
  waiting for transfers between devices  109 us (32%)
  blocking collectives  60.8 us (18%)
  matrix products  34.5 us (10%)
  between operations  13.5 us (4%)
    add x31, other arithmetic, combine_states(): summed = summed_a * factor_a[:, :, None] + summed_b * factor_b[:, :, None]  110 us
    all_gather x1, waiting for transfers between devices, combined_all(): lax.all_gather(a.astype(kind), axis)  62.6 us
    all_gather x2, blocking collectives, combined_all(): lax.all_gather(a.astype(kind), axis)  47 us
    all_gather x1, waiting for transfers between devices, local(): whole = lax.all_gather(absorb(queries, key_up), 'ctx', axis=0, tiled=True)  46.7 us
    psum x1, blocking collectives, local(): return lax.psum(partial_out, 'heads').astype(jnp.bfloat16)  13.8 us
    dot_general x1, matrix products, attend(): jnp.einsum('ilv,ivz->ilz', weight.astype(jnp.bfloat16), latent_store_cach...  12 us
    dot_general x1, matrix products, attend(): jnp.einsum('str,sdr->std', request_query, latent_store_cache, preferred_e...  11 us
  transfers between devices with their start and end apart: 2, of which 2 were waited for; matrix products, arithmetic and copies ran while one was open for 1% of the time, Pallas kernels for 0%

commit v1 on v0

v1 whole, which is shorter than its diff:
```python
import functools
import math

import jax
import jax.numpy as jnp
from jax import lax
from jax.experimental import pallas as pl
from jax.experimental.pallas import tpu as pltpu
from jax.sharding import PartitionSpec as P

NEG = -3e38
MESH = pl.DeviceIdType.MESH
F32 = jnp.float32
BF16 = jnp.bfloat16


def kernel(
    n,
    groups,
    reqs,
    queries,
    cache,
    fresh,
    lengths,
    key_up,
    value_up,
    out_proj,
    out,
    kc,
    ku,
    vu,
    op,
    nl,
    qg,
    qn,
    qrope,
    ql,
    qfull,
    osum,
    stat,
    sbuf,
    sstat,
    rbuf,
    rstat,
    ho,
    hg,
    xb,
    cache_sem,
    local_sem,
    q_send,
    q_recv,
    p_send,
    p_recv,
    t_send,
    t_recv,
    h_send,
    h_recv,
    x_send,
    x_recv,
):
    me = lax.axis_index("ctx")
    group = lax.axis_index("heads")
    rows = n
    heads = key_up.shape[0]
    nope = key_up.shape[1]
    latent = key_up.shape[2]
    chunks = latent // 128
    width = cache.shape[2]
    keys = cache.shape[1]
    steps = rows // reqs
    per = steps * heads
    coef = math.log2(math.e) / math.sqrt(queries.shape[2])

    def peer(i):
        return lax.rem(me + 1 + i, n)

    own_q = pltpu.make_async_copy(queries.at[0], qg.at[me], local_sem.at[0])
    get_ku = pltpu.make_async_copy(key_up, ku, local_sem.at[1])
    get_vu = pltpu.make_async_copy(value_up, vu, local_sem.at[2])
    get_op = pltpu.make_async_copy(out_proj, op, local_sem.at[3])
    get_nl = pltpu.make_async_copy(fresh, nl, local_sem.at[4])
    own_q.start()
    get_nl.start()
    get_ku.start()

    def get_cache(b):
        return pltpu.make_async_copy(cache.at[b], kc.at[b], cache_sem.at[b])

    for b in range(reqs):
        get_cache(b).start()
    get_vu.start()
    get_op.start()

    barrier = pltpu.get_barrier_semaphore()

    @pl.loop(0, n - 1)
    def _(i):
        pl.semaphore_signal(barrier, inc=1, device_id={"ctx": peer(i)}, device_id_type=MESH)

    for i in range(1, groups):
        pl.semaphore_signal(
            barrier, inc=1, device_id={"heads": lax.rem(group + i, groups)}, device_id_type=MESH
        )
    pl.semaphore_wait(barrier, n - 1 + groups - 1)

    def send_q(to, slot):
        return pltpu.make_async_remote_copy(
            src_ref=queries.at[0],
            dst_ref=qg.at[slot],
            send_sem=q_send.at[to],
            recv_sem=q_recv.at[slot],
            device_id={"ctx": to},
            device_id_type=MESH,
        )

    @pl.loop(0, n - 1)
    def _(i):
        send_q(peer(i), me).start()

    own_q.wait()

    @pl.loop(0, n - 1)
    def _(i):
        send_q(peer(i), peer(i)).wait_recv()

    @pl.loop(0, rows)
    def _(r):
        block = qg[r]
        at = pl.ds(pl.multiple_of(r * heads, heads), heads)
        qn[at, :] = block[:, :nope].astype(F32)
        qrope[at, : width - latent] = block[:, nope:].astype(F32)
        qfull[at, latent:] = block[:, nope:]

    get_ku.wait()

    @pl.loop(0, heads)
    def _(h):
        x = qn[pl.ds(h, rows, stride=heads), :].astype(BF16)
        y = jnp.dot(x, ku[h], preferred_element_type=F32)
        for c in range(chunks):
            ql[c, pl.ds(h, rows, stride=heads), :] = y[:, c * 128 : (c + 1) * 128]

    @pl.loop(0, reqs)
    def _(b):
        at = pl.ds(pl.multiple_of(b * per, per), per)
        for c in range(chunks):
            qfull[at, c * 128 : (c + 1) * 128] = ql[c, at, :].astype(BF16)

    @pl.loop(0, reqs)
    def _(b):
        get_cache(b).wait()
        at = pl.ds(pl.multiple_of(b * per, per), per)
        s = lax.dot_general(
            qfull[at, :], kc[b], (((1,), (1,)), ((), ())), preferred_element_type=F32
        )
        position = me * keys + lax.broadcasted_iota(jnp.int32, (1, keys), 1)
        s = jnp.where(position < lengths[b], s, NEG)
        m = jnp.max(s, axis=1, keepdims=True)
        p = jnp.exp2((s - m) * coef)
        total = jnp.sum(p, axis=1, keepdims=True)
        o = jnp.dot(p.astype(BF16), kc[b, :, :latent], preferred_element_type=F32)
        for c in range(chunks):
            osum[c, at, :] = o[:, c * 128 : (c + 1) * 128]
        lane = lax.broadcasted_iota(jnp.int32, (per, 128), 1)
        stat[at, :] = jnp.where(lane < rows, m, total)

    get_vu.wait()

    def send_p(to, slot):
        return (
            pltpu.make_async_remote_copy(
                src_ref=sbuf.at[to],
                dst_ref=rbuf.at[slot],
                send_sem=p_send.at[to],
                recv_sem=p_recv.at[slot],
                device_id={"ctx": to},
                device_id_type=MESH,
            ),
            pltpu.make_async_remote_copy(
                src_ref=sstat.at[to],
                dst_ref=rstat.at[slot],
                send_sem=t_send.at[to],
                recv_sem=t_recv.at[slot],
                device_id={"ctx": to},
                device_id_type=MESH,
            ),
        )

    row_of = lax.broadcasted_iota(jnp.int32, (rows, 128), 0)
    lane_of = lax.broadcasted_iota(jnp.int32, (rows, 128), 1)
    diagonal = (lane_of < 2 * rows) & (lax.rem(lane_of, rows) == row_of)

    def partial_of(h):
        x = jnp.concatenate(
            [osum[c, pl.ds(h, rows, stride=heads), :] for c in range(chunks)], axis=1
        ).astype(BF16)
        y = jnp.dot(x, vu[h], preferred_element_type=F32).astype(BF16)
        t = jnp.where(diagonal, stat[pl.ds(h, rows, stride=heads), :], 0.0)
        return y, jnp.sum(t, axis=0, keepdims=True)

    @pl.loop(0, n - 1)
    def _(i):
        h = peer(i)
        y, t = partial_of(h)
        sbuf[h] = y
        sstat[h] = t
        for copy in send_p(h, me):
            copy.start()

    y, t = partial_of(me)
    rbuf[me] = y
    rstat[me] = t

    get_nl.wait()
    mine = jnp.concatenate(
        [ql[c, pl.ds(me, rows, stride=heads), :] for c in range(chunks)], axis=1
    ).astype(BF16)
    mine_rope = qrope[pl.ds(me, rows, stride=heads), :][:, : width - latent].astype(BF16)
    contract = (((1,), (1,)), ((), ()))
    near = lax.dot_general(mine, nl[:, :latent], contract, preferred_element_type=F32)
    near = near + lax.dot_general(mine_rope, nl[:, latent:], contract, preferred_element_type=F32)
    row = lax.broadcasted_iota(jnp.int32, (rows, rows), 0)
    col = lax.broadcasted_iota(jnp.int32, (rows, rows), 1)
    seen = (row // steps == col // steps) & (col <= row)
    near = jnp.where(seen, near, NEG)
    top_near = jnp.max(near, axis=1, keepdims=True)
    w_near = jnp.exp2((near - top_near) * coef)
    total_near = jnp.sum(w_near, axis=1, keepdims=True)
    o_near = jnp.dot(w_near.astype(BF16), nl[:, :latent], preferred_element_type=F32)
    y_near = jnp.dot(o_near.astype(BF16), vu[me], preferred_element_type=F32)

    @pl.loop(0, n - 1)
    def _(i):
        for copy in send_p(peer(i), peer(i)):
            copy.wait_recv()

    turned = jnp.transpose(rstat[:, 0, :])
    tops = turned[:rows, :]
    totals = turned[rows : 2 * rows, :]
    top = jnp.maximum(jnp.max(tops, axis=1, keepdims=True), top_near)
    factor = jnp.exp2((tops - top) * coef)
    factor_near = jnp.exp2((top_near - top) * coef)
    total = jnp.sum(factor * totals, axis=1, keepdims=True) + factor_near * total_near
    acc = y_near * factor_near
    for s in range(n):
        acc = acc + rbuf[s].astype(F32) * factor[:, s : s + 1]
    done = (acc / total).astype(BF16)
    ho[...] = done
    hg[:, pl.ds(pl.multiple_of(me * 128, 128), 128)] = done

    def send_h(to, slot):
        return pltpu.make_async_remote_copy(
            src_ref=ho,
            dst_ref=hg.at[:, pl.ds(pl.multiple_of(slot * 128, 128), 128)],
            send_sem=h_send.at[to],
            recv_sem=h_recv.at[slot],
            device_id={"ctx": to},
            device_id_type=MESH,
        )

    @pl.loop(0, n - 1)
    def _(i):
        send_h(peer(i), me).start()

    get_op.wait()

    @pl.loop(0, n - 1)
    def _(i):
        send_h(peer(i), peer(i)).wait_recv()

    xb[group] = jnp.dot(hg[...], op[...], preferred_element_type=F32)

    def send_x(to, slot):
        return pltpu.make_async_remote_copy(
            src_ref=xb.at[group],
            dst_ref=xb.at[slot],
            send_sem=x_send.at[to],
            recv_sem=x_recv.at[slot],
            device_id={"heads": to},
            device_id_type=MESH,
        )

    for i in range(1, groups):
        send_x(lax.rem(group + i, groups), group).start()
    for i in range(1, groups):
        other = lax.rem(group + i, groups)
        send_x(other, other).wait_recv()
    result = xb[0]
    for g in range(1, groups):
        result = result + xb[g]
    out[...] = result.astype(out.dtype)

    @pl.loop(0, n - 1)
    def _(i):
        to = peer(i)
        send_q(to, me).wait_send()
        for copy in send_p(to, me):
            copy.wait_send()
        send_h(to, me).wait_send()

    for i in range(1, groups):
        send_x(lax.rem(group + i, groups), group).wait_send()


def local(n, groups, queries, cache, fresh, lengths, key_up, value_up, out_proj):
    heads, nope, latent = key_up.shape
    reqs, keys, width = cache.shape
    rows = fresh.shape[0]
    vdim = value_up.shape[2]
    columns = out_proj.shape[1]
    chunks = latent // 128
    hbm = pl.BlockSpec(memory_space=pl.ANY)
    dma = pltpu.SemaphoreType.DMA
    return pl.pallas_call(
        functools.partial(kernel, n, groups, reqs),
        out_shape=jax.ShapeDtypeStruct((rows, columns), BF16),
        in_specs=[hbm, hbm, hbm, pl.BlockSpec(memory_space=pltpu.SMEM), hbm, hbm, hbm],
        out_specs=pl.BlockSpec(memory_space=pltpu.VMEM),
        scratch_shapes=[
            pltpu.VMEM((reqs, keys, width), BF16),
            pltpu.VMEM((heads, nope, latent), BF16),
            pltpu.VMEM((heads, latent, vdim), BF16),
            pltpu.VMEM((heads * vdim, columns), BF16),
            pltpu.VMEM((rows, width), BF16),
            pltpu.VMEM((rows, heads, queries.shape[2]), BF16),
            pltpu.VMEM((rows * heads, nope), F32),
            pltpu.VMEM((rows * heads, 128), F32),
            pltpu.VMEM((chunks, rows * heads, 128), F32),
            pltpu.VMEM((rows * heads, width), BF16),
            pltpu.VMEM((chunks, rows * heads, 128), F32),
            pltpu.VMEM((rows * heads, 128), F32),
            pltpu.VMEM((heads, rows, vdim), BF16),
            pltpu.VMEM((heads, 1, 128), F32),
            pltpu.VMEM((n, rows, vdim), BF16),
            pltpu.VMEM((n, 1, 128), F32),
            pltpu.VMEM((rows, vdim), BF16),
            pltpu.VMEM((rows, heads * vdim), BF16),
            pltpu.VMEM((groups, rows, columns), F32),
            dma((reqs,)),
            dma((5,)),
            dma((n,)),
            dma((n,)),
            dma((n,)),
            dma((n,)),
            dma((n,)),
            dma((n,)),
            dma((n,)),
            dma((n,)),
            dma((groups,)),
            dma((groups,)),
        ],
        compiler_params=pltpu.CompilerParams(
            collective_id=0, has_side_effects=True, vmem_limit_bytes=56 * 1024 * 1024
        ),
        cost_estimate=pl.CostEstimate(
            flops=4 * 10**9, bytes_accessed=25 * 10**6, transcendentals=2 * 10**6
        ),
        name="mla_decode",
    )(queries, cache, fresh, lengths, key_up, value_up, out_proj)


def solution(mesh):
    in_specs = (
        P("ctx", "heads", None),
        P(None, "ctx", None),
        P(),
        P(),
        P("heads", None, None),
        P("heads", None, None),
        P("heads", "ctx"),
    )
    body = functools.partial(local, mesh.shape["ctx"], mesh.shape["heads"])
    return jax.shard_map(
        body, mesh=mesh, in_specs=in_specs, out_specs=P(None, "ctx"), check_vma=False
    )
```

time: 344 us -> 85.6 us (0.25)
  other arithmetic: 121 us -> 0 us
  waiting for transfers between devices: 109 us -> 0 us
  Pallas kernels: 0 us -> 60.9 us
  blocking collectives: 60.8 us -> 0 us
  matrix products: 34.5 us -> 0 us
  local copies, waits for them, and re-layouts: 1.89 us -> 24.1 us
  between operations: 13.5 us -> 0.01 us
    add x63 -> x0, other arithmetic: 111 us -> none  [the longest x31 110 us: combine_states(): summed = summed_a * factor_a[:, :, None] + summed_b * factor_b[:, :, None]]
    all_gather x2 -> x0, waiting for transfers between devices: 109 us -> none  [the longest x1 62.6 us: combined_all(): lax.all_gather(a.astype(kind), axis)]
    pallas_call x0 -> x1, Pallas kernels: none -> 60.9 us  [local(): pl.pallas_call(functools.partial(kernel, n, groups, reqs), out_shape=jax....]
    all_gather x2 -> x0, blocking collectives: 47 us -> none  [combined_all(): lax.all_gather(a.astype(kind), axis)]
    dot_general x7 -> x0, matrix products: 34.5 us -> none  [the longest x1 12 us: attend(): jnp.einsum('ilv,ivz->ilz', weight.astype(jnp.bfloat16), latent_store_cach...]
    unnamed x8 -> x3, local copies, waits for them, and re-layouts: 0.87 us -> 24.1 us
    psum x1 -> x0, blocking collectives: 13.8 us -> none  [local(): return lax.psum(partial_out, 'heads').astype(jnp.bfloat16)]
    reduce_sum x2 -> x0, other arithmetic: 4.53 us -> none  [attend(): total = jnp.sum(weight, axis=2) + jnp.sum(weight_near, axis=2)]
  transfers between devices with their start and end apart: 2 -> 0, of which waited for: 2 -> 0; matrix products, arithmetic and copies ran while one was open for 1% -> 0% of each run, Pallas kernels for 0% -> 0%
where the time goes in v1:
time: 85.6 us; the launch traced here: 84.9 us
  Pallas kernels  60.9 us (71%)
  local copies, waits for them, and re-layouts  24.1 us (28%)
    pallas_call x1, Pallas kernels, local(): pl.pallas_call(functools.partial(kernel, n, groups, reqs), out_shape=jax....  60.9 us
    unnamed x3, local copies, waits for them, and re-layouts  24.1 us

profile of v1, /device:TPU:1, one launch (start us, length us, event | category | flops | bytes accessed | tf_op | source)
XLA Modules:
  0.0 84.9 jit_solution(5034734438094740436)
XLA Ops:
  0.0 4.0 %copy.9.out_proj = bf16[4096,224]{1,0:T(8,128)(2,1)} copy(bf16[4096,224]{0,1:T(8,128)(2,1)} %param.13) | data formatting | bytes 3670016 | tf_op args[6]
  4.0 18.7 %copy.8.cache = bf16[8,1536,576]{2,1,0:T(8,128)(2,1)} copy(bf16[8,1536,576]{1,2,0:T(8,128)(2,1)} %param.8) | data formatting | bytes 28311552 | tf_op args[1]
  22.7 60.9 %mla_decode.1 = bf16[32,224]{1,0:T(8,128)(2,1)} custom-call(bf16[1,32,192]{2,1,0:T(8,128)(2,1)} %queries.1, bf16[8,1536,576]{2,1,0:T(8,128)(2,1)} %copy.8.cache, bf16[32,576]{1,0:T(8,128)(2,1)} %fresh.1, s32[8]{0:T(128)} %lengths.1, bf16[32,128,512]{2,1,0:T(8,128)(2,1)} %key_up.1, bf16[32,512,128]{2,1,0:T(8,128)(2,1)} %value_up.1, ...), custom_call_target="tpu_custom_call" | custom-call | flops 4000000000 | bytes 25000000 | tf_op jit(solution)/shard_map/mla_decode/pallas_call | solution.py:314
  83.6 1.3 %copy.11 = bf16[32,224]{1,0:T(8,128)(2,1)} copy(bf16[32,224]{1,0:T(8,128)(2,1)} %mla_decode.1) | data formatting | bytes 28672

commit v2 on v1

--- a/solution.py
+++ b/solution.py
@@ -65,10 +65,11 @@
     nope = key_up.shape[1]
     latent = key_up.shape[2]
     chunks = latent // 128
-    width = cache.shape[2]
-    keys = cache.shape[1]
+    width = cache.shape[1]
+    keys = cache.shape[2]
     steps = rows // reqs
     per = steps * heads
+    contract = (((1,), (1,)), ((), ()))
     coef = math.log2(math.e) / math.sqrt(queries.shape[2])
 
     def peer(i):
@@ -150,15 +151,15 @@
     def _(b):
         get_cache(b).wait()
         at = pl.ds(pl.multiple_of(b * per, per), per)
-        s = lax.dot_general(
-            qfull[at, :], kc[b], (((1,), (1,)), ((), ())), preferred_element_type=F32
-        )
+        s = jnp.dot(qfull[at, :], kc[b], preferred_element_type=F32)
         position = me * keys + lax.broadcasted_iota(jnp.int32, (1, keys), 1)
         s = jnp.where(position < lengths[b], s, NEG)
         m = jnp.max(s, axis=1, keepdims=True)
         p = jnp.exp2((s - m) * coef)
         total = jnp.sum(p, axis=1, keepdims=True)
-        o = jnp.dot(p.astype(BF16), kc[b, :, :latent], preferred_element_type=F32)
+        o = lax.dot_general(
+            p.astype(BF16), kc[b, :latent, :], contract, preferred_element_type=F32
+        )
         for c in range(chunks):
             osum[c, at, :] = o[:, c * 128 : (c + 1) * 128]
         lane = lax.broadcasted_iota(jnp.int32, (per, 128), 1)
@@ -216,7 +217,6 @@
         [ql[c, pl.ds(me, rows, stride=heads), :] for c in range(chunks)], axis=1
     ).astype(BF16)
     mine_rope = qrope[pl.ds(me, rows, stride=heads), :][:, : width - latent].astype(BF16)
-    contract = (((1,), (1,)), ((), ()))
     near = lax.dot_general(mine, nl[:, :latent], contract, preferred_element_type=F32)
     near = near + lax.dot_general(mine_rope, nl[:, latent:], contract, preferred_element_type=F32)
     row = lax.broadcasted_iota(jnp.int32, (rows, rows), 0)
@@ -268,7 +268,7 @@
     def _(i):
         send_h(peer(i), peer(i)).wait_recv()
 
-    xb[group] = jnp.dot(hg[...], op[...], preferred_element_type=F32)
+    xb[group] = lax.dot_general(hg[...], op[...], contract, preferred_element_type=F32)
 
     def send_x(to, slot):
         return pltpu.make_async_remote_copy(
@@ -303,11 +303,13 @@
 
 
 def local(n, groups, queries, cache, fresh, lengths, key_up, value_up, out_proj):
+    cache = jnp.swapaxes(cache, 1, 2)
+    out_proj = jnp.swapaxes(out_proj, 0, 1)
     heads, nope, latent = key_up.shape
-    reqs, keys, width = cache.shape
+    reqs, width, keys = cache.shape
     rows = fresh.shape[0]
     vdim = value_up.shape[2]
-    columns = out_proj.shape[1]
+    columns = out_proj.shape[0]
     chunks = latent // 128
     hbm = pl.BlockSpec(memory_space=pl.ANY)
     dma = pltpu.SemaphoreType.DMA
@@ -317,10 +319,10 @@
         in_specs=[hbm, hbm, hbm, pl.BlockSpec(memory_space=pltpu.SMEM), hbm, hbm, hbm],
         out_specs=pl.BlockSpec(memory_space=pltpu.VMEM),
         scratch_shapes=[
-            pltpu.VMEM((reqs, keys, width), BF16),
+            pltpu.VMEM((reqs, width, keys), BF16),
             pltpu.VMEM((heads, nope, latent), BF16),
             pltpu.VMEM((heads, latent, vdim), BF16),
-            pltpu.VMEM((heads * vdim, columns), BF16),
+            pltpu.VMEM((columns, heads * vdim), BF16),
             pltpu.VMEM((rows, width), BF16),
             pltpu.VMEM((rows, heads, queries.shape[2]), BF16),
             pltpu.VMEM((rows * heads, nope), F32),

time: 85.6 us -> 61.8 us (0.72)
  local copies, waits for them, and re-layouts: 24.1 us -> 1.32 us
    unnamed x3 -> x1, local copies, waits for them, and re-layouts: 24.1 us -> 1.32 us
where the time goes in v2:
time: 61.8 us; the launch traced here: 61.6 us
  Pallas kernels  60.3 us (98%)
  local copies, waits for them, and re-layouts  1.32 us (2%)
    pallas_call x1, Pallas kernels, local(): pl.pallas_call(functools.partial(kernel, n, groups, reqs), out_shape=jax....  60.3 us
    unnamed x1, local copies, waits for them, and re-layouts  1.32 us

profile of v2, /device:TPU:1, one launch (start us, length us, event | category | flops | bytes accessed | tf_op | source)
XLA Modules:
  0.0 61.6 jit_solution(17924576568865857274)
XLA Ops:
  0.0 60.3 %mla_decode.1 = bf16[32,224]{1,0:T(8,128)(2,1)} custom-call(bf16[1,32,192]{2,1,0:T(8,128)(2,1)} %queries.1, bf16[8,576,1536]{2,1,0:T(8,128)(2,1)} %bitcast.2, bf16[32,576]{1,0:T(8,128)(2,1)} %fresh.1, s32[8]{0:T(128)} %lengths.1, bf16[32,128,512]{2,1,0:T(8,128)(2,1)} %key_up.1, bf16[32,512,128]{2,1,0:T(8,128)(2,1)} %value_up.1, bf16[224,4096]{1,0:T(8,128)(2,1)} %bitcast.3), custom_call_target="tpu_custom_call" | custom-call | flops 4000000000 | bytes 25000000 | tf_op jit(solution)/shard_map/mla_decode/pallas_call | solution.py:316
  60.3 1.3 %copy.9 = bf16[32,224]{1,0:T(8,128)(2,1)} copy(bf16[32,224]{1,0:T(8,128)(2,1)} %mla_decode.1) | data formatting | bytes 28672

commit v3 on v2

v3 whole, which is shorter than its diff:
```python
import functools
import math

import jax
import jax.numpy as jnp
from jax import lax
from jax.experimental import pallas as pl
from jax.experimental.pallas import tpu as pltpu
from jax.sharding import PartitionSpec as P

NEG = -3e38
MESH = pl.DeviceIdType.MESH
F32 = jnp.float32
BF16 = jnp.bfloat16
SIDE = 4
LANES = 128


def widen(f):
    halves = []
    for u in range(2):
        halves.append(
            jnp.concatenate(
                [jnp.broadcast_to(f[:, u * 8 + k : u * 8 + k + 1], (8, LANES)) for k in range(8)],
                axis=1,
            )
        )
    return jnp.concatenate(halves, axis=0)


def kernel(
    groups,
    queries,
    cache,
    fresh,
    lengths,
    key_up,
    value_up,
    out_proj,
    out,
    kc,
    ku,
    vu,
    op,
    nl,
    qg,
    qfull,
    perm,
    st,
    stl,
    sr,
    srl,
    cb,
    cbl,
    rb,
    rbl,
    ho,
    hg,
    xb,
    cache_sem,
    local_sem,
    q_send,
    q_recv,
    s_send,
    s_recv,
    r_send,
    r_recv,
    h_send,
    h_recv,
    f_send,
    f_recv,
    x_send,
    x_recv,
):
    me = lax.axis_index("ctx")
    group = lax.axis_index("heads")
    core = lax.rem(me, 2)
    z = lax.rem(me // 2, SIDE)
    y = me // (2 * SIDE)
    rows = fresh.shape[0]
    heads, nope, latent = key_up.shape
    reqs, width, keys = cache.shape
    steps = rows // reqs
    per = steps * heads
    coef = math.log2(math.e) / math.sqrt(queries.shape[2])
    contract = (((1,), (1,)), ((), ()))

    def at(dy, dz, dc=0):
        return (
            lax.rem(y + dy, SIDE) * (2 * SIDE) + lax.rem(z + dz, SIDE) * 2 + lax.rem(core + dc, 2)
        )

    sibling = at(0, 0, 1)
    others = [(dy, dz) for dy in range(SIDE) for dz in range(SIDE) if dy or dz]

    own_q = pltpu.make_async_copy(queries.at[0], qg.at[me], local_sem.at[0])
    get_ku = pltpu.make_async_copy(key_up, ku, local_sem.at[1])
    get_vu = pltpu.make_async_copy(value_up, vu, local_sem.at[2])
    get_op = pltpu.make_async_copy(out_proj, op, local_sem.at[3])
    get_nl = pltpu.make_async_copy(fresh, nl, local_sem.at[4])

    def get_cache(b):
        return pltpu.make_async_copy(cache.at[b], kc.at[b], cache_sem.at[b])

    own_q.start()
    get_nl.start()
    get_ku.start()
    for u in range(2):
        get_cache(2 * y + u).start()
    get_vu.start()

    @pl.loop(2, reqs)
    def _(i):
        get_cache(lax.rem(2 * y + i, reqs)).start()

    get_op.start()

    barrier = pltpu.get_barrier_semaphore()
    rings = [sibling]
    for d in range(1, SIDE):
        rings += [at(0, d), at(d, 0)]
    for to in rings:
        pl.semaphore_signal(barrier, inc=1, device_id={"ctx": to}, device_id_type=MESH)
    for i in range(1, groups):
        pl.semaphore_signal(
            barrier, inc=1, device_id={"heads": lax.rem(group + i, groups)}, device_id_type=MESH
        )
    to_row = lax.broadcasted_iota(jnp.int32, (2 * per, 2 * per), 0)
    of_row = lax.broadcasted_iota(jnp.int32, (2 * per, 2 * per), 1)
    perm[...] = jnp.where(
        of_row == lax.rem(to_row, 2 * steps) * heads + to_row // (2 * steps), 1.0, 0.0
    ).astype(BF16)
    own_q.wait()
    pl.semaphore_wait(barrier, len(rings) + groups - 1)

    def send_q(to, row, k):
        return pltpu.make_async_remote_copy(
            src_ref=qg.at[row],
            dst_ref=qg.at[row],
            send_sem=q_send.at[k],
            recv_sem=q_recv.at[row],
            device_id={"ctx": to},
            device_id_type=MESH,
        )

    q_sends = []
    for d in (1, 3, 2):
        q_sends.append((at(0, d), me))
    for d in (1, 3, 2):
        q_sends.append((at(d, 0), me))
    q_sends.append((sibling, me))
    for dz in (1, 3, 2):
        for d in (1, 3, 2):
            q_sends.append((at(d, 0), at(0, dz)))
        q_sends.append((sibling, at(0, dz)))
    for dy in (1, 3, 2):
        for dz in (0, 1, 3, 2):
            q_sends.append((sibling, at(dy, dz)))
    q_sends = [send_q(to, row, k) for k, (to, row) in enumerate(q_sends)]

    def got_q(row):
        send_q(sibling, row, 0).wait_recv()

    for k in range(7):
        q_sends[k].start()
    for i, dz in enumerate((1, 3, 2)):
        got_q(at(0, dz))
        for k in range(4):
            q_sends[7 + 4 * i + k].start()
    for dz in range(SIDE):
        got_q(at(0, dz, 1))

    sub = lax.broadcasted_iota(jnp.int32, (8, LANES), 0)

    def absorb(pairs):
        starts = [pl.multiple_of(j * 8, 8) for j in pairs]
        many = 8 * len(pairs)
        which = lax.broadcasted_iota(jnp.int32, (many, 8, LANES), 1)
        for two in range(heads // 16):
            span = slice(two * 16, two * 16 + 16)
            x = jnp.concatenate([qg[pl.ds(s, 8), span, :nope] for s in starts], axis=0).astype(F32)
            halves = []
            for u in range(2):
                part = x[:, u * 8 : u * 8 + 8, :]
                wide = jnp.concatenate(
                    [
                        jnp.where(which == k, part, 0.0).reshape(many * 8, LANES).astype(BF16)
                        for k in range(8)
                    ],
                    axis=1,
                )
                first = two * 16 + u * 8
                w = ku[first : first + 8].reshape(8 * nope, latent)
                halves.append(
                    jnp.dot(wide, w, preferred_element_type=F32).reshape(many, 8, latent)
                )
            lat = jnp.concatenate(halves, axis=1).astype(BF16)
            for i, s in enumerate(starts):
                qfull[pl.ds(s, 8), span, :latent] = lat[i * 8 : i * 8 + 8]
        for s in starts:
            qfull[pl.ds(s, 8), :, latent:] = qg[pl.ds(s, 8), :, nope:]

    position = me * keys + lax.broadcasted_iota(jnp.int32, (1, keys), 1)

    def attend(b, near):
        q = qfull[pl.ds(b * steps, steps)].reshape(per, width)
        s = jnp.dot(q, kc[b], preferred_element_type=F32)
        s = jnp.where(position < lengths[b], s, NEG)
        m = jnp.max(s, axis=1, keepdims=True)
        if near:
            n_s = lax.dot_general(q, nl[...], contract, preferred_element_type=F32)
            row = b * steps + lax.broadcasted_iota(jnp.int32, n_s.shape, 0) // heads
            key = lax.broadcasted_iota(jnp.int32, n_s.shape, 1)
            seen = (key >= b * steps) & (key <= row) & (lax.rem(me, 2 * SIDE) == 0)
            n_s = jnp.where(seen, n_s, NEG)
            m = jnp.maximum(m, jnp.max(n_s, axis=1, keepdims=True))
        p = jnp.exp2((s - m) * coef)
        total = jnp.sum(p, axis=1, keepdims=True)
        o = lax.dot_general(
            p.astype(BF16), kc[b, :latent, :], contract, preferred_element_type=F32
        )
        if near:
            n_p = jnp.where(seen, jnp.exp2((n_s - m) * coef), 0.0)
            total = total + jnp.sum(n_p, axis=1, keepdims=True)
            o = o + jnp.dot(n_p.astype(BF16), nl[:, :latent], preferred_element_type=F32)
        return (o / total).astype(BF16), m * coef + jnp.log2(total)

    def to_sibling(p):
        return (
            pltpu.make_async_remote_copy(
                src_ref=st.at[p, 1 - core],
                dst_ref=sr.at[p],
                send_sem=s_send.at[p],
                recv_sem=s_recv.at[p],
                device_id={"ctx": sibling},
                device_id_type=MESH,
            ),
            pltpu.make_async_remote_copy(
                src_ref=stl.at[p, 1 - core],
                dst_ref=srl.at[p],
                send_sem=s_send.at[SIDE + p],
                recv_sem=s_recv.at[SIDE + p],
                device_id={"ctx": sibling},
                device_id_type=MESH,
            ),
        )

    def pair_of(p):
        return lax.rem(y + p, SIDE)

    def work(p, near):
        j = pair_of(p)
        done = []
        for u in range(2):
            get_cache(2 * j + u).wait()
            done.append(attend(2 * j + u, near))
        o = jnp.concatenate([d[0] for d in done], axis=0)
        turned = jnp.dot(perm[...], o, preferred_element_type=F32).astype(BF16)
        log = jnp.concatenate([d[1] for d in done], axis=0)
        h_of = lax.rem(lax.broadcasted_iota(jnp.int32, (2 * per, LANES), 0), heads)
        lane = lax.broadcasted_iota(jnp.int32, (2 * per, LANES), 1)
        log = jnp.sum(jnp.where(h_of == lane, log, 0.0).reshape(8, heads, LANES), axis=1)
        stl[p, 0] = log
        stl[p, 1] = pltpu.roll(log, LANES - 16, 1)
        blocks = []
        for g in range(heads // 8):
            w = jnp.concatenate([vu[g * 8 + k] for k in range(8)], axis=1)
            r = jnp.dot(turned[g * 64 : g * 64 + 64], w, preferred_element_type=F32)
            blocks.append(
                jnp.concatenate(
                    [r[k * 8 : k * 8 + 8, k * LANES : (k + 1) * LANES] for k in range(8)], axis=1
                )
            )
        for c in range(2):
            st[p, c] = jnp.concatenate(blocks[2 * c : 2 * c + 2], axis=0).astype(BF16)
        for copy in to_sibling(p):
            copy.start()

    def to_owner(p, dy):
        j = pair_of(p)
        to_y = lax.rem(y + dy, SIDE)
        to = to_y * (2 * SIDE) + j * 2 + core
        return (
            pltpu.make_async_remote_copy(
                src_ref=cb.at[p, to_y],
                dst_ref=rb.at[me // 2],
                send_sem=r_send.at[p * SIDE + dy],
                recv_sem=r_recv.at[me // 2],
                device_id={"ctx": to},
                device_id_type=MESH,
            ),
            pltpu.make_async_remote_copy(
                src_ref=cbl.at[p],
                dst_ref=rbl.at[me // 2],
                send_sem=r_send.at[16 + p * SIDE + dy],
                recv_sem=r_recv.at[16 + me // 2],
                device_id={"ctx": to},
                device_id_type=MESH,
            ),
        )

    def join(p):
        for copy in to_sibling(p):
            copy.wait_recv()
        la, lb = stl[p, core], srl[p]
        top = jnp.maximum(la, lb)
        wa, wb = jnp.exp2(la - top), jnp.exp2(lb - top)
        both = wa + wb
        cbl[p] = top + jnp.log2(both)
        o = st[p, core].astype(F32) * widen(wa / both) + sr[p].astype(F32) * widen(wb / both)
        o = o.astype(BF16)
        for i in range(SIDE):
            cb[p, i] = o[:, i * 256 : i * 256 + 256]
        mine = pair_of(p) == z

        @pl.when(mine)
        def _():
            rb[me // 2] = cb[p, y]
            rbl[me // 2] = cbl[p]

        @pl.when(jnp.logical_not(mine))
        def _():
            for copy in to_owner(p, 0):
                copy.start()

        for dy in (1, 3, 2):
            for copy in to_owner(p, dy):
                copy.start()

    get_ku.wait()
    absorb([y])
    get_vu.wait()
    get_nl.wait()
    work(0, True)

    k = 19
    for dy in (1, 3, 2):
        for dz in (0, 1, 3, 2):
            got_q(at(dy, dz))
            q_sends[k].start()
            k += 1
    for dy in (1, 3, 2):
        for dz in range(SIDE):
            got_q(at(dy, dz, 1))
    absorb([pair_of(p) for p in range(1, SIDE)])

    @pl.loop(1, SIDE)
    def _(p):
        work(p, False)
        join(p - 1)

    join(SIDE - 1)

    def from_owner(source):
        return (
            pltpu.make_async_remote_copy(
                src_ref=cb.at[0, 0],
                dst_ref=rb.at[source],
                send_sem=r_send.at[0],
                recv_sem=r_recv.at[source],
                device_id={"ctx": sibling},
                device_id_type=MESH,
            ),
            pltpu.make_async_remote_copy(
                src_ref=cbl.at[0],
                dst_ref=rbl.at[source],
                send_sem=r_send.at[0],
                recv_sem=r_recv.at[16 + source],
                device_id={"ctx": sibling},
                device_id_type=MESH,
            ),
        )

    for dy, dz in others:
        for copy in from_owner(at(dy, dz) // 2):
            copy.wait_recv()

    logs = rbl[...]
    top = jnp.max(logs, axis=0)
    w = jnp.exp2(logs - top[None])
    w = w / jnp.sum(w, axis=0)[None]
    acc = jnp.zeros((16, 256), F32)
    for s in range(SIDE * SIDE):
        f = pltpu.roll(w[s], lax.rem(LANES - 2 * y, LANES), 1)
        f = [jnp.broadcast_to(f[:, i : i + 1], (8, LANES)) for i in (0, 1, 8, 9)]
        f = jnp.concatenate(
            [jnp.concatenate(f[:2], axis=1), jnp.concatenate(f[2:], axis=1)], axis=0
        )
        acc = acc + rb[s].astype(F32) * f
    ho[...] = acc.astype(BF16)
    hg[core, z, y] = ho[...]

    def send_h(to, source):
        return pltpu.make_async_remote_copy(
            src_ref=ho,
            dst_ref=hg.at[core, lax.rem(source, SIDE), source // SIDE],
            send_sem=h_send.at[to // 2],
            recv_sem=h_recv.at[source],
            device_id={"ctx": to},
            device_id_type=MESH,
        )

    def forward(of_core, dz):
        slot = lax.rem(z + dz, SIDE)
        return pltpu.make_async_remote_copy(
            src_ref=hg.at[of_core, slot],
            dst_ref=hg.at[of_core, slot],
            send_sem=f_send.at[dz],
            recv_sem=f_recv.at[slot],
            device_id={"ctx": sibling},
            device_id_type=MESH,
        )

    for dy, dz in others:
        send_h(at(dy, dz), me // 2).start()
    for dz in (0, 1, 3, 2):
        for dy in range(SIDE):
            if dy or dz:
                send_h(at(dy, dz), at(dy, dz) // 2).wait_recv()
        forward(core, dz).start()
    get_op.wait()
    for dz in range(SIDE):
        forward(1 - core, dz).wait_recv()

    total = jnp.zeros((rows, out.shape[1]), F32)
    for c in range(2):
        for i in range(SIDE):
            x = [hg[c, pair, i].astype(F32) for pair in range(SIDE)]
            for u in range(2):
                lhs = jnp.concatenate([a[u * 8 : u * 8 + 8] for a in x], axis=0).astype(BF16)
                first = (c * 16 + u * 8 + i * 2) * LANES
                total = total + lax.dot_general(
                    lhs, op[:, first : first + 256], contract, preferred_element_type=F32
                )
    xb[group] = total

    def send_x(to, slot):
        return pltpu.make_async_remote_copy(
            src_ref=xb.at[group],
            dst_ref=xb.at[slot],
            send_sem=x_send.at[to],
            recv_sem=x_recv.at[slot],
            device_id={"heads": to},
            device_id_type=MESH,
        )

    for i in range(1, groups):
        send_x(lax.rem(group + i, groups), group).start()
    for i in range(1, groups):
        other = lax.rem(group + i, groups)
        send_x(other, other).wait_recv()
    result = xb[0]
    for g in range(1, groups):
        result = result + xb[g]
    out[...] = result.astype(out.dtype)

    for copy in q_sends:
        copy.wait_send()
    for p in range(SIDE):
        for copy in to_sibling(p):
            copy.wait_send()

        @pl.when(pair_of(p) != z)
        def _(p=p):
            for copy in to_owner(p, 0):
                copy.wait_send()

        for dy in range(1, SIDE):
            for copy in to_owner(p, dy):
                copy.wait_send()
    for dy, dz in others:
        send_h(at(dy, dz), me // 2).wait_send()
    for dz in range(SIDE):
        forward(core, dz).wait_send()
    for i in range(1, groups):
        send_x(lax.rem(group + i, groups), group).wait_send()


def local(groups, queries, cache, fresh, lengths, key_up, value_up, out_proj):
    cache = jnp.swapaxes(cache, 1, 2)
    out_proj = jnp.swapaxes(out_proj, 0, 1)
    heads, nope, latent = key_up.shape
    reqs, width, keys = cache.shape
    rows = fresh.shape[0]
    vdim = value_up.shape[2]
    columns = out_proj.shape[0]
    per = rows // reqs * heads
    chips = SIDE * SIDE
    hbm = pl.BlockSpec(memory_space=pl.ANY)
    dma = pltpu.SemaphoreType.DMA
    return pl.pallas_call(
        functools.partial(kernel, groups),
        out_shape=jax.ShapeDtypeStruct((rows, columns), BF16),
        in_specs=[hbm, hbm, hbm, pl.BlockSpec(memory_space=pltpu.SMEM), hbm, hbm, hbm],
        out_specs=pl.BlockSpec(memory_space=pltpu.VMEM),
        scratch_shapes=[
            pltpu.VMEM((reqs, width, keys), BF16),
            pltpu.VMEM((heads, nope, latent), BF16),
            pltpu.VMEM((heads, latent, vdim), BF16),
            pltpu.VMEM((columns, heads * vdim), BF16),
            pltpu.VMEM((rows, width), BF16),
            pltpu.VMEM((rows, heads, queries.shape[2]), BF16),
            pltpu.VMEM((rows, heads, width), BF16),
            pltpu.VMEM((2 * per, 2 * per), BF16),
            pltpu.VMEM((SIDE, 2, 16, 1024), BF16),
            pltpu.VMEM((SIDE, 2, 8, LANES), F32),
            pltpu.VMEM((SIDE, 16, 1024), BF16),
            pltpu.VMEM((SIDE, 8, LANES), F32),
            pltpu.VMEM((SIDE, SIDE, 16, 256), BF16),
            pltpu.VMEM((SIDE, 8, LANES), F32),
            pltpu.VMEM((chips, 16, 256), BF16),
            pltpu.VMEM((chips, 8, LANES), F32),
            pltpu.VMEM((16, 256), BF16),
            pltpu.VMEM((2, SIDE, SIDE, 16, 256), BF16),
            pltpu.VMEM((groups, rows, columns), F32),
            dma((reqs,)),
            dma((5,)),
            dma((31,)),
            dma((rows,)),
            dma((2 * SIDE,)),
            dma((2 * SIDE,)),
            dma((2 * chips,)),
            dma((2 * chips,)),
            dma((chips,)),
            dma((chips,)),
            dma((SIDE,)),
            dma((SIDE,)),
            dma((groups,)),
            dma((groups,)),
        ],
        compiler_params=pltpu.CompilerParams(
            collective_id=0, has_side_effects=True, vmem_limit_bytes=56 * 1024 * 1024
        ),
        cost_estimate=pl.CostEstimate(
            flops=4 * 10**9, bytes_accessed=25 * 10**6, transcendentals=2 * 10**6
        ),
        name="mla_decode",
    )(queries, cache, fresh, lengths, key_up, value_up, out_proj)


def solution(mesh):
    in_specs = (
        P("ctx", "heads", None),
        P(None, "ctx", None),
        P(),
        P(),
        P("heads", None, None),
        P("heads", None, None),
        P("heads", "ctx"),
    )
    body = functools.partial(local, mesh.shape["heads"])
    return jax.shard_map(
        body, mesh=mesh, in_specs=in_specs, out_specs=P(None, "ctx"), check_vma=False
    )
```

time: 61.8 us -> 51.3 us (0.83)
  Pallas kernels: 60.3 us -> 49.7 us
    pallas_call x1, Pallas kernels: 60.3 us -> 49.7 us  [local(): pl.pallas_call(functools.partial(kernel, groups), out_shape=jax.ShapeDtyp...]
where the time goes in v3:
time: 51.3 us; the launch traced here: 51.1 us
  Pallas kernels  49.7 us (97%)
  local copies, waits for them, and re-layouts  1.32 us (3%)
    pallas_call x1, Pallas kernels, local(): pl.pallas_call(functools.partial(kernel, groups), out_shape=jax.ShapeDtyp...  49.7 us
    unnamed x1, local copies, waits for them, and re-layouts  1.32 us

profile of v3, /device:TPU:1, one launch (start us, length us, event | category | flops | bytes accessed | tf_op | source)
XLA Modules:
  0.0 51.1 jit_solution(12138210273058027003)
XLA Ops:
  0.0 49.7 %mla_decode.1 = bf16[32,224]{1,0:T(8,128)(2,1)} custom-call(bf16[1,32,192]{2,1,0:T(8,128)(2,1)} %queries.1, bf16[8,576,1536]{2,1,0:T(8,128)(2,1)} %bitcast.2, bf16[32,576]{1,0:T(8,128)(2,1)} %fresh.1, s32[8]{0:T(128)} %lengths.1, bf16[32,128,512]{2,1,0:T(8,128)(2,1)} %key_up.1, bf16[32,512,128]{2,1,0:T(8,128)(2,1)} %value_up.1, bf16[224,4096]{1,0:T(8,128)(2,1)} %bitcast.3), custom_call_target="tpu_custom_call" | custom-call | flops 4000000000 | bytes 25000000 | tf_op jit(solution)/shard_map/mla_decode/pallas_call | solution.py:491
  49.7 1.3 %copy.9 = bf16[32,224]{1,0:T(8,128)(2,1)} copy(bf16[32,224]{1,0:T(8,128)(2,1)} %mla_decode.1) | data formatting | bytes 28672

commit v4 on v3

--- a/solution.py
+++ b/solution.py
@@ -33,7 +33,7 @@
     queries,
     cache,
     fresh,
-    lengths,
+    lengths_in,
     key_up,
     value_up,
     out_proj,
@@ -43,9 +43,14 @@
     vu,
     op,
     nl,
+    lengths,
+    qown,
     qg,
     qfull,
     perm,
+    ot,
+    tops,
+    sums,
     st,
     stl,
     sr,
@@ -93,26 +98,28 @@
     sibling = at(0, 0, 1)
     others = [(dy, dz) for dy in range(SIDE) for dz in range(SIDE) if dy or dz]
 
-    own_q = pltpu.make_async_copy(queries.at[0], qg.at[me], local_sem.at[0])
+    own_q = pltpu.make_async_copy(queries.at[0], qown, local_sem.at[0])
     get_ku = pltpu.make_async_copy(key_up, ku, local_sem.at[1])
     get_vu = pltpu.make_async_copy(value_up, vu, local_sem.at[2])
     get_op = pltpu.make_async_copy(out_proj, op, local_sem.at[3])
     get_nl = pltpu.make_async_copy(fresh, nl, local_sem.at[4])
+    get_lengths = pltpu.make_async_copy(lengths_in, lengths, local_sem.at[5])
 
     def get_cache(b):
         return pltpu.make_async_copy(cache.at[b], kc.at[b], cache_sem.at[b])
 
     own_q.start()
     get_nl.start()
+    get_lengths.start()
     get_ku.start()
     for u in range(2):
         get_cache(2 * y + u).start()
-    get_vu.start()
 
     @pl.loop(2, reqs)
     def _(i):
         get_cache(lax.rem(2 * y + i, reqs)).start()
 
+    get_vu.start()
     get_op.start()
 
     barrier = pltpu.get_barrier_semaphore()
@@ -128,9 +135,14 @@
     to_row = lax.broadcasted_iota(jnp.int32, (2 * per, 2 * per), 0)
     of_row = lax.broadcasted_iota(jnp.int32, (2 * per, 2 * per), 1)
     perm[...] = jnp.where(
-        of_row == lax.rem(to_row, 2 * steps) * heads + to_row // (2 * steps), 1.0, 0.0
+        of_row == (to_row & (2 * steps - 1)) * heads + to_row // (2 * steps), 1.0, 0.0
     ).astype(BF16)
     own_q.wait()
+    rope = width - latent
+    half = heads // 2
+    qg[me, :heads] = qown[:, :nope]
+    qg[me, heads:] = jnp.concatenate([qown[:half, nope:], qown[half:, nope:]], axis=1)
+    get_lengths.wait()
     pl.semaphore_wait(barrier, len(rings) + groups - 1)
 
     def send_q(to, row, k):
@@ -149,12 +161,16 @@
     for d in (1, 3, 2):
         q_sends.append((at(d, 0), me))
     q_sends.append((sibling, me))
-    for dz in (1, 3, 2):
+    near_rows = [at(d * core, d * (1 - core)) for d in (1, 3, 2)]
+    far_rows = [at(d * (1 - core), d * core) for d in (1, 3, 2)]
+    for row in near_rows:
         for d in (1, 3, 2):
-            q_sends.append((at(d, 0), at(0, dz)))
-        q_sends.append((sibling, at(0, dz)))
+            q_sends.append((at(d * (1 - core), d * core), row))
+        q_sends.append((sibling, row))
+    for row in far_rows:
+        q_sends.append((sibling, row))
     for dy in (1, 3, 2):
-        for dz in (0, 1, 3, 2):
+        for dz in (1, 3, 2):
             q_sends.append((sibling, at(dy, dz)))
     q_sends = [send_q(to, row, k) for k, (to, row) in enumerate(q_sends)]
 
@@ -163,14 +179,15 @@
 
     for k in range(7):
         q_sends[k].start()
-    for i, dz in enumerate((1, 3, 2)):
-        got_q(at(0, dz))
+    for i, row in enumerate(near_rows):
+        got_q(row)
         for k in range(4):
             q_sends[7 + 4 * i + k].start()
+    for i, row in enumerate(far_rows):
+        got_q(row)
+        q_sends[19 + i].start()
     for dz in range(SIDE):
         got_q(at(0, dz, 1))
-
-    sub = lax.broadcasted_iota(jnp.int32, (8, LANES), 0)
 
     def absorb(pairs):
         starts = [pl.multiple_of(j * 8, 8) for j in pairs]
@@ -178,7 +195,7 @@
         which = lax.broadcasted_iota(jnp.int32, (many, 8, LANES), 1)
         for two in range(heads // 16):
             span = slice(two * 16, two * 16 + 16)
-            x = jnp.concatenate([qg[pl.ds(s, 8), span, :nope] for s in starts], axis=0).astype(F32)
+            x = jnp.concatenate([qg[pl.ds(s, 8), span, :] for s in starts], axis=0).astype(F32)
             halves = []
             for u in range(2):
                 part = x[:, u * 8 : u * 8 + 8, :]
@@ -198,7 +215,8 @@
             for i, s in enumerate(starts):
                 qfull[pl.ds(s, 8), span, :latent] = lat[i * 8 : i * 8 + 8]
         for s in starts:
-            qfull[pl.ds(s, 8), :, latent:] = qg[pl.ds(s, 8), :, nope:]
+            qfull[pl.ds(s, 8), :half, latent:] = qg[pl.ds(s, 8), heads:, :rope]
+            qfull[pl.ds(s, 8), half:, latent:] = qg[pl.ds(s, 8), heads:, rope:]
 
     position = me * keys + lax.broadcasted_iota(jnp.int32, (1, keys), 1)
 
@@ -217,13 +235,15 @@
         p = jnp.exp2((s - m) * coef)
         total = jnp.sum(p, axis=1, keepdims=True)
         o = lax.dot_general(
-            p.astype(BF16), kc[b, :latent, :], contract, preferred_element_type=F32
+            kc[b, :latent, :], p.astype(BF16), contract, preferred_element_type=F32
         )
         if near:
             n_p = jnp.where(seen, jnp.exp2((n_s - m) * coef), 0.0)
             total = total + jnp.sum(n_p, axis=1, keepdims=True)
-            o = o + jnp.dot(n_p.astype(BF16), nl[:, :latent], preferred_element_type=F32)
-        return (o / total).astype(BF16), m * coef + jnp.log2(total)
+            o = o + lax.dot_general(
+                nl[:, :latent], n_p.astype(BF16), (((0,), (1,)), ((), ())), preferred_element_type=F32
+            )
+        return o.astype(BF16), m * coef, total
 
     def to_sibling(p):
         return (
@@ -248,33 +268,47 @@
     def pair_of(p):
         return lax.rem(y + p, SIDE)
 
-    def work(p, near):
-        j = pair_of(p)
-        done = []
-        for u in range(2):
-            get_cache(2 * j + u).wait()
-            done.append(attend(2 * j + u, near))
-        o = jnp.concatenate([d[0] for d in done], axis=0)
-        turned = jnp.dot(perm[...], o, preferred_element_type=F32).astype(BF16)
-        log = jnp.concatenate([d[1] for d in done], axis=0)
-        h_of = lax.rem(lax.broadcasted_iota(jnp.int32, (2 * per, LANES), 0), heads)
-        lane = lax.broadcasted_iota(jnp.int32, (2 * per, LANES), 1)
-        log = jnp.sum(jnp.where(h_of == lane, log, 0.0).reshape(8, heads, LANES), axis=1)
-        stl[p, 0] = log
-        stl[p, 1] = pltpu.roll(log, LANES - 16, 1)
-        blocks = []
+    head_of = lax.broadcasted_iota(jnp.int32, (per, LANES), 0) & (heads - 1)
+    lane_of = lax.broadcasted_iota(jnp.int32, (per, LANES), 1)
+    lane = lax.broadcasted_iota(jnp.int32, (8, LANES), 1)
+
+    def spread(column):
+        one = jnp.where(head_of == lane_of, column, 0.0).reshape(steps, heads, LANES)
+        return jnp.sum(one, axis=1)
+
+    def work(p, u, near):
+        b = 2 * pair_of(p) + u
+        o, m, total = attend(b, near)
+        ot[p, :, u * per : (u + 1) * per] = o
+        tops[p, u * steps : (u + 1) * steps, :] = spread(m)
+        sums[p, u * steps : (u + 1) * steps, :] = spread(total)
+
+    def project(pairs):
+        turned = []
+        for p in pairs:
+            t = lax.dot_general(perm[...], ot[p], contract, preferred_element_type=F32)
+            turned.append(t.astype(BF16))
+            a, b = tops[p], sums[p]
+            stl[p, 0] = jnp.where(lane < 16, a, pltpu.roll(b, 16, 1))
+            stl[p, 1] = jnp.where(lane < 16, pltpu.roll(a, LANES - 16, 1), b)
+        blocks = [[] for _ in pairs]
         for g in range(heads // 8):
             w = jnp.concatenate([vu[g * 8 + k] for k in range(8)], axis=1)
-            r = jnp.dot(turned[g * 64 : g * 64 + 64], w, preferred_element_type=F32)
-            blocks.append(
-                jnp.concatenate(
-                    [r[k * 8 : k * 8 + 8, k * LANES : (k + 1) * LANES] for k in range(8)], axis=1
+            x = jnp.concatenate([t[g * 64 : g * 64 + 64] for t in turned], axis=0)
+            r = jnp.dot(x, w, preferred_element_type=F32)
+            for i in range(len(pairs)):
+                part = r[i * 64 : i * 64 + 64]
+                blocks[i].append(
+                    jnp.concatenate(
+                        [part[k * 8 : k * 8 + 8, k * LANES : (k + 1) * LANES] for k in range(8)],
+                        axis=1,
+                    )
                 )
-            )
-        for c in range(2):
-            st[p, c] = jnp.concatenate(blocks[2 * c : 2 * c + 2], axis=0).astype(BF16)
-        for copy in to_sibling(p):
-            copy.start()
+        for i, p in enumerate(pairs):
+            for c in range(2):
+                st[p, c] = jnp.concatenate(blocks[i][2 * c : 2 * c + 2], axis=0).astype(BF16)
+            for copy in to_sibling(p):
+                copy.start()
 
     def to_owner(p, dy):
         j = pair_of(p)
@@ -305,7 +339,7 @@
         la, lb = stl[p, core], srl[p]
         top = jnp.maximum(la, lb)
         wa, wb = jnp.exp2(la - top), jnp.exp2(lb - top)
-        both = wa + wb
+        both = wa * pltpu.roll(la, LANES - 16, 1) + wb * pltpu.roll(lb, LANES - 16, 1)
         cbl[p] = top + jnp.log2(both)
         o = st[p, core].astype(F32) * widen(wa / both) + sr[p].astype(F32) * widen(wb / both)
         o = o.astype(BF16)
@@ -328,14 +362,18 @@
                 copy.start()
 
     get_ku.wait()
+    for b in range(reqs):
+        get_cache(b).wait()
+    get_vu.wait()
+    get_op.wait()
     absorb([y])
-    get_vu.wait()
     get_nl.wait()
-    work(0, True)
-
-    k = 19
+    work(0, 0, True)
+    work(0, 1, True)
+
+    k = 22
     for dy in (1, 3, 2):
-        for dz in (0, 1, 3, 2):
+        for dz in (1, 3, 2):
             got_q(at(dy, dz))
             q_sends[k].start()
             k += 1
@@ -344,11 +382,17 @@
             got_q(at(dy, dz, 1))
     absorb([pair_of(p) for p in range(1, SIDE)])
 
-    @pl.loop(1, SIDE)
+    @pl.loop(1, SIDE - 1)
     def _(p):
-        work(p, False)
-        join(p - 1)
-
+        work(p, 0, False)
+        work(p, 1, False)
+
+    project(range(SIDE - 1))
+    work(SIDE - 1, 0, False)
+    for p in range(SIDE - 1):
+        join(p)
+    work(SIDE - 1, 1, False)
+    project([SIDE - 1])
     join(SIDE - 1)
 
     def from_owner(source):
@@ -418,7 +462,6 @@
             if dy or dz:
                 send_h(at(dy, dz), at(dy, dz) // 2).wait_recv()
         forward(core, dz).start()
-    get_op.wait()
     for dz in range(SIDE):
         forward(1 - core, dz).wait_recv()
 
@@ -432,7 +475,7 @@
                 total = total + lax.dot_general(
                     lhs, op[:, first : first + 256], contract, preferred_element_type=F32
                 )
-    xb[group] = total
+    xb[group] = total.astype(BF16)
 
     def send_x(to, slot):
         return pltpu.make_async_remote_copy(
@@ -449,9 +492,9 @@
     for i in range(1, groups):
         other = lax.rem(group + i, groups)
         send_x(other, other).wait_recv()
-    result = xb[0]
+    result = xb[0].astype(F32)
     for g in range(1, groups):
-        result = result + xb[g]
+        result = result + xb[g].astype(F32)
     out[...] = result.astype(out.dtype)
 
     for copy in q_sends:
@@ -491,7 +534,7 @@
     return pl.pallas_call(
         functools.partial(kernel, groups),
         out_shape=jax.ShapeDtypeStruct((rows, columns), BF16),
-        in_specs=[hbm, hbm, hbm, pl.BlockSpec(memory_space=pltpu.SMEM), hbm, hbm, hbm],
+        in_specs=[hbm] * 7,
         out_specs=pl.BlockSpec(memory_space=pltpu.VMEM),
         scratch_shapes=[
             pltpu.VMEM((reqs, width, keys), BF16),
@@ -499,9 +542,14 @@
             pltpu.VMEM((heads, latent, vdim), BF16),
             pltpu.VMEM((columns, heads * vdim), BF16),
             pltpu.VMEM((rows, width), BF16),
-            pltpu.VMEM((rows, heads, queries.shape[2]), BF16),
+            pltpu.SMEM((reqs,), jnp.int32),
+            pltpu.VMEM((heads, queries.shape[2]), BF16),
+            pltpu.VMEM((rows, heads + heads // 2, LANES), BF16),
             pltpu.VMEM((rows, heads, width), BF16),
             pltpu.VMEM((2 * per, 2 * per), BF16),
+            pltpu.VMEM((SIDE, latent, 2 * per), BF16),
+            pltpu.VMEM((SIDE, 8, LANES), F32),
+            pltpu.VMEM((SIDE, 8, LANES), F32),
             pltpu.VMEM((SIDE, 2, 16, 1024), BF16),
             pltpu.VMEM((SIDE, 2, 8, LANES), F32),
             pltpu.VMEM((SIDE, 16, 1024), BF16),
@@ -512,9 +560,9 @@
             pltpu.VMEM((chips, 8, LANES), F32),
             pltpu.VMEM((16, 256), BF16),
             pltpu.VMEM((2, SIDE, SIDE, 16, 256), BF16),
-            pltpu.VMEM((groups, rows, columns), F32),
+            pltpu.VMEM((groups, rows, columns), BF16),
             dma((reqs,)),
-            dma((5,)),
+            dma((6,)),
             dma((31,)),
             dma((rows,)),
             dma((2 * SIDE,)),

time: 51.3 us -> 49.6 us (0.967)
  Pallas kernels: 49.7 us -> 48 us
    pallas_call x1, Pallas kernels: 49.7 us -> 48 us  [local(): pl.pallas_call(functools.partial(kernel, groups), out_shape=jax.ShapeDtyp...]
where the time goes in v4:
time: 49.6 us; the launch traced here: 49.4 us
  Pallas kernels  48 us (97%)
  local copies, waits for them, and re-layouts  1.32 us (3%)
    pallas_call x1, Pallas kernels, local(): pl.pallas_call(functools.partial(kernel, groups), out_shape=jax.ShapeDtyp...  48 us
    unnamed x1, local copies, waits for them, and re-layouts  1.32 us

profile of v4, /device:TPU:1, one launch (start us, length us, event | category | flops | bytes accessed | tf_op | source)
XLA Modules:
  0.0 49.4 jit_solution(5683837326677837014)
XLA Ops:
  0.0 48.0 %mla_decode.1 = bf16[32,224]{1,0:T(8,128)(2,1)} custom-call(bf16[1,32,192]{2,1,0:T(8,128)(2,1)} %queries.1, bf16[8,576,1536]{2,1,0:T(8,128)(2,1)} %bitcast.2, bf16[32,576]{1,0:T(8,128)(2,1)} %fresh.1, s32[8]{0:T(128)} %lengths_in.1, bf16[32,128,512]{2,1,0:T(8,128)(2,1)} %key_up.1, bf16[32,512,128]{2,1,0:T(8,128)(2,1)} %value_up.1, bf16[224,4096]{1,0:T(8,128)(2,1)} %bitcast.3), custom_call_target="tpu_custom_call" | custom-call | flops 4000000000 | bytes 25000000 | tf_op jit(solution)/shard_map/mla_decode/pallas_call | solution.py:534
  48.0 1.3 %copy.9 = bf16[32,224]{1,0:T(8,128)(2,1)} copy(bf16[32,224]{1,0:T(8,128)(2,1)} %mla_decode.1) | data formatting | bytes 28672

commit v5 on v4

--- a/solution.py
+++ b/solution.py
@@ -39,6 +39,7 @@
     out_proj,
     out,
     kc,
+    vt,
     ku,
     vu,
     op,
@@ -123,10 +124,8 @@
     get_op.start()
 
     barrier = pltpu.get_barrier_semaphore()
-    rings = [sibling]
-    for d in range(1, SIDE):
-        rings += [at(0, d), at(d, 0)]
-    for to in rings:
+    peers = [sibling] + [at(dy, dz) for dy, dz in others]
+    for to in peers:
         pl.semaphore_signal(barrier, inc=1, device_id={"ctx": to}, device_id_type=MESH)
     for i in range(1, groups):
         pl.semaphore_signal(
@@ -143,7 +142,7 @@
     qg[me, :heads] = qown[:, :nope]
     qg[me, heads:] = jnp.concatenate([qown[:half, nope:], qown[half:, nope:]], axis=1)
     get_lengths.wait()
-    pl.semaphore_wait(barrier, len(rings) + groups - 1)
+    pl.semaphore_wait(barrier, len(peers) + groups - 1)
 
     def send_q(to, row, k):
         return pltpu.make_async_remote_copy(
@@ -155,37 +154,31 @@
             device_id_type=MESH,
         )
 
-    q_sends = []
-    for d in (1, 3, 2):
-        q_sends.append((at(0, d), me))
-    for d in (1, 3, 2):
-        q_sends.append((at(d, 0), me))
-    q_sends.append((sibling, me))
-    near_rows = [at(d * core, d * (1 - core)) for d in (1, 3, 2)]
-    far_rows = [at(d * (1 - core), d * core) for d in (1, 3, 2)]
-    for row in near_rows:
-        for d in (1, 3, 2):
-            q_sends.append((at(d * (1 - core), d * core), row))
-        q_sends.append((sibling, row))
-    for row in far_rows:
-        q_sends.append((sibling, row))
-    for dy in (1, 3, 2):
-        for dz in (1, 3, 2):
-            q_sends.append((sibling, at(dy, dz)))
+    along_z = [(0, 1), (0, 3), (0, 2)]
+    across = [(2, 2), (2, 1), (2, 3), (1, 2), (3, 2), (1, 1), (1, 3), (3, 1), (3, 3)]
+    across += [(2, 0), (1, 0), (3, 0)]
+    q_sends = [(sibling, me)] + [(at(dy, dz), me) for dy, dz in along_z + across]
+    q_sends += [(sibling, at(dy, dz)) for dy, dz in along_z + across[::-1]]
     q_sends = [send_q(to, row, k) for k, (to, row) in enumerate(q_sends)]
 
     def got_q(row):
         send_q(sibling, row, 0).wait_recv()
 
-    for k in range(7):
+    for k in range(16):
         q_sends[k].start()
-    for i, row in enumerate(near_rows):
-        got_q(row)
-        for k in range(4):
-            q_sends[7 + 4 * i + k].start()
-    for i, row in enumerate(far_rows):
-        got_q(row)
-        q_sends[19 + i].start()
+
+    @pl.loop(0, reqs)
+    def _(i):
+        b = lax.rem(2 * y + i, reqs)
+        get_cache(b).wait()
+        for c in range(latent // LANES):
+            vt[b, :, c * LANES : (c + 1) * LANES] = jnp.transpose(
+                kc[b, c * LANES : (c + 1) * LANES, :]
+            )
+
+    for i, (dy, dz) in enumerate(along_z):
+        got_q(at(dy, dz))
+        q_sends[16 + i].start()
     for dz in range(SIDE):
         got_q(at(0, dz, 1))
 
@@ -234,15 +227,11 @@
             m = jnp.maximum(m, jnp.max(n_s, axis=1, keepdims=True))
         p = jnp.exp2((s - m) * coef)
         total = jnp.sum(p, axis=1, keepdims=True)
-        o = lax.dot_general(
-            kc[b, :latent, :], p.astype(BF16), contract, preferred_element_type=F32
-        )
+        o = jnp.dot(p.astype(BF16), vt[b], preferred_element_type=F32)
         if near:
             n_p = jnp.where(seen, jnp.exp2((n_s - m) * coef), 0.0)
             total = total + jnp.sum(n_p, axis=1, keepdims=True)
-            o = o + lax.dot_general(
-                nl[:, :latent], n_p.astype(BF16), (((0,), (1,)), ((), ())), preferred_element_type=F32
-            )
+            o = o + jnp.dot(n_p.astype(BF16), nl[:, :latent], preferred_element_type=F32)
         return o.astype(BF16), m * coef, total
 
     def to_sibling(p):
@@ -279,14 +268,14 @@
     def work(p, u, near):
         b = 2 * pair_of(p) + u
         o, m, total = attend(b, near)
-        ot[p, :, u * per : (u + 1) * per] = o
+        ot[p, u * per : (u + 1) * per, :] = o
         tops[p, u * steps : (u + 1) * steps, :] = spread(m)
         sums[p, u * steps : (u + 1) * steps, :] = spread(total)
 
     def project(pairs):
         turned = []
         for p in pairs:
-            t = lax.dot_general(perm[...], ot[p], contract, preferred_element_type=F32)
+            t = jnp.dot(perm[...], ot[p], preferred_element_type=F32)
             turned.append(t.astype(BF16))
             a, b = tops[p], sums[p]
             stl[p, 0] = jnp.where(lane < 16, a, pltpu.roll(b, 16, 1))
@@ -362,26 +351,19 @@
                 copy.start()
 
     get_ku.wait()
-    for b in range(reqs):
-        get_cache(b).wait()
+    get_nl.wait()
     get_vu.wait()
     get_op.wait()
     absorb([y])
-    get_nl.wait()
+    for i, (dy, dz) in enumerate(across[::-1]):
+        got_q(at(dy, dz))
+        q_sends[19 + i].start()
     work(0, 0, True)
-    work(0, 1, True)
-
-    k = 22
-    for dy in (1, 3, 2):
-        for dz in (1, 3, 2):
-            got_q(at(dy, dz))
-            q_sends[k].start()
-            k += 1
-    for dy in (1, 3, 2):
+    for dy in range(1, SIDE):
         for dz in range(SIDE):
             got_q(at(dy, dz, 1))
     absorb([pair_of(p) for p in range(1, SIDE)])
-
+    work(0, 1, True)
     @pl.loop(1, SIDE - 1)
     def _(p):
         work(p, 0, False)
@@ -538,6 +520,7 @@
         out_specs=pl.BlockSpec(memory_space=pltpu.VMEM),
         scratch_shapes=[
             pltpu.VMEM((reqs, width, keys), BF16),
+            pltpu.VMEM((reqs, keys, latent), BF16),
             pltpu.VMEM((heads, nope, latent), BF16),
             pltpu.VMEM((heads, latent, vdim), BF16),
             pltpu.VMEM((columns, heads * vdim), BF16),
@@ -547,7 +530,7 @@
             pltpu.VMEM((rows, heads + heads // 2, LANES), BF16),
             pltpu.VMEM((rows, heads, width), BF16),
             pltpu.VMEM((2 * per, 2 * per), BF16),
-            pltpu.VMEM((SIDE, latent, 2 * per), BF16),
+            pltpu.VMEM((SIDE, 2 * per, latent), BF16),
             pltpu.VMEM((SIDE, 8, LANES), F32),
             pltpu.VMEM((SIDE, 8, LANES), F32),
             pltpu.VMEM((SIDE, 2, 16, 1024), BF16),

time: 49.6 us -> 47 us (0.948)
  Pallas kernels: 48 us -> 45.4 us
    pallas_call x1, Pallas kernels: 48 us -> 45.4 us  [local(): pl.pallas_call(functools.partial(kernel, groups), out_shape=jax.ShapeDtyp...]
where the time goes in v5:
time: 47 us; the launch traced here: 46.7 us
  Pallas kernels  45.4 us (97%)
  local copies, waits for them, and re-layouts  1.32 us (3%)
    pallas_call x1, Pallas kernels, local(): pl.pallas_call(functools.partial(kernel, groups), out_shape=jax.ShapeDtyp...  45.4 us
    unnamed x1, local copies, waits for them, and re-layouts  1.32 us

profile of v5, /device:TPU:1, one launch (start us, length us, event | category | flops | bytes accessed | tf_op | source)
XLA Modules:
  0.0 46.7 jit_solution(5824263584406977791)
XLA Ops:
  0.0 45.4 %mla_decode.1 = bf16[32,224]{1,0:T(8,128)(2,1)} custom-call(bf16[1,32,192]{2,1,0:T(8,128)(2,1)} %queries.1, bf16[8,576,1536]{2,1,0:T(8,128)(2,1)} %bitcast.2, bf16[32,576]{1,0:T(8,128)(2,1)} %fresh.1, s32[8]{0:T(128)} %lengths_in.1, bf16[32,128,512]{2,1,0:T(8,128)(2,1)} %key_up.1, bf16[32,512,128]{2,1,0:T(8,128)(2,1)} %value_up.1, bf16[224,4096]{1,0:T(8,128)(2,1)} %bitcast.3), custom_call_target="tpu_custom_call" | custom-call | flops 4000000000 | bytes 25000000 | tf_op jit(solution)/shard_map/mla_decode/pallas_call | solution.py:516
  45.4 1.3 %copy.9 = bf16[32,224]{1,0:T(8,128)(2,1)} copy(bf16[32,224]{1,0:T(8,128)(2,1)} %mla_decode.1) | data formatting | bytes 28672

commit v6 on v5

--- a/solution.py
+++ b/solution.py
@@ -14,18 +14,6 @@
 BF16 = jnp.bfloat16
 SIDE = 4
 LANES = 128
-
-
-def widen(f):
-    halves = []
-    for u in range(2):
-        halves.append(
-            jnp.concatenate(
-                [jnp.broadcast_to(f[:, u * 8 + k : u * 8 + k + 1], (8, LANES)) for k in range(8)],
-                axis=1,
-            )
-        )
-    return jnp.concatenate(halves, axis=0)
 
 
 def kernel(
@@ -54,10 +42,6 @@
     sums,
     st,
     stl,
-    sr,
-    srl,
-    cb,
-    cbl,
     rb,
     rbl,
     ho,
@@ -67,14 +51,10 @@
     local_sem,
     q_send,
     q_recv,
-    s_send,
-    s_recv,
     r_send,
     r_recv,
     h_send,
     h_recv,
-    f_send,
-    f_recv,
     x_send,
     x_recv,
 ):
@@ -98,6 +78,9 @@
 
     sibling = at(0, 0, 1)
     others = [(dy, dz) for dy in range(SIDE) for dz in range(SIDE) if dy or dz]
+    hops = (0, 1, 2, 1)
+    everyone = [(dy, dz, dc) for dy, dz in [(0, 0)] + others for dc in range(2) if dy or dz or dc]
+    everyone.sort(key=lambda d: -hops[d[0]] - hops[d[1]])
 
     own_q = pltpu.make_async_copy(queries.at[0], qown, local_sem.at[0])
     get_ku = pltpu.make_async_copy(key_up, ku, local_sem.at[1])
@@ -234,26 +217,6 @@
             o = o + jnp.dot(n_p.astype(BF16), nl[:, :latent], preferred_element_type=F32)
         return o.astype(BF16), m * coef, total
 
-    def to_sibling(p):
-        return (
-            pltpu.make_async_remote_copy(
-                src_ref=st.at[p, 1 - core],
-                dst_ref=sr.at[p],
-                send_sem=s_send.at[p],
-                recv_sem=s_recv.at[p],
-                device_id={"ctx": sibling},
-                device_id_type=MESH,
-            ),
-            pltpu.make_async_remote_copy(
-                src_ref=stl.at[p, 1 - core],
-                dst_ref=srl.at[p],
-                send_sem=s_send.at[SIDE + p],
-                recv_sem=s_recv.at[SIDE + p],
-                device_id={"ctx": sibling},
-                device_id_type=MESH,
-            ),
-        )
-
     def pair_of(p):
         return lax.rem(y + p, SIDE)
 
@@ -271,6 +234,32 @@
         ot[p, u * per : (u + 1) * per, :] = o
         tops[p, u * steps : (u + 1) * steps, :] = spread(m)
         sums[p, u * steps : (u + 1) * steps, :] = spread(total)
+
+    owners = [(2, 0), (2, 1), (1, 0), (1, 1), (3, 0), (3, 1), (0, 1)]
+
+    def to_owner(p, dy, dc):
+        to_y = lax.rem(y + dy, SIDE)
+        to_core = lax.rem(core + dc, 2)
+        to = to_y * (2 * SIDE) + pair_of(p) * 2 + to_core
+        k = (p * SIDE + dy) * 2 + dc
+        return (
+            pltpu.make_async_remote_copy(
+                src_ref=st.at[p, to_core, to_y],
+                dst_ref=rb.at[me],
+                send_sem=r_send.at[k],
+                recv_sem=r_recv.at[me],
+                device_id={"ctx": to},
+                device_id_type=MESH,
+            ),
+            pltpu.make_async_remote_copy(
+                src_ref=stl.at[p, to_core],
+                dst_ref=rbl.at[me],
+                send_sem=r_send.at[rows + k],
+                recv_sem=r_recv.at[rows + me],
+                device_id={"ctx": to},
+                device_id_type=MESH,
+            ),
+        )
 
     def project(pairs):
         turned = []
@@ -295,60 +284,24 @@
                 )
         for i, p in enumerate(pairs):
             for c in range(2):
-                st[p, c] = jnp.concatenate(blocks[i][2 * c : 2 * c + 2], axis=0).astype(BF16)
-            for copy in to_sibling(p):
-                copy.start()
-
-    def to_owner(p, dy):
-        j = pair_of(p)
-        to_y = lax.rem(y + dy, SIDE)
-        to = to_y * (2 * SIDE) + j * 2 + core
-        return (
-            pltpu.make_async_remote_copy(
-                src_ref=cb.at[p, to_y],
-                dst_ref=rb.at[me // 2],
-                send_sem=r_send.at[p * SIDE + dy],
-                recv_sem=r_recv.at[me // 2],
-                device_id={"ctx": to},
-                device_id_type=MESH,
-            ),
-            pltpu.make_async_remote_copy(
-                src_ref=cbl.at[p],
-                dst_ref=rbl.at[me // 2],
-                send_sem=r_send.at[16 + p * SIDE + dy],
-                recv_sem=r_recv.at[16 + me // 2],
-                device_id={"ctx": to},
-                device_id_type=MESH,
-            ),
-        )
-
-    def join(p):
-        for copy in to_sibling(p):
-            copy.wait_recv()
-        la, lb = stl[p, core], srl[p]
-        top = jnp.maximum(la, lb)
-        wa, wb = jnp.exp2(la - top), jnp.exp2(lb - top)
-        both = wa * pltpu.roll(la, LANES - 16, 1) + wb * pltpu.roll(lb, LANES - 16, 1)
-        cbl[p] = top + jnp.log2(both)
-        o = st[p, core].astype(F32) * widen(wa / both) + sr[p].astype(F32) * widen(wb / both)
-        o = o.astype(BF16)
-        for i in range(SIDE):
-            cb[p, i] = o[:, i * 256 : i * 256 + 256]
-        mine = pair_of(p) == z
-
-        @pl.when(mine)
-        def _():
-            rb[me // 2] = cb[p, y]
-            rbl[me // 2] = cbl[p]
-
-        @pl.when(jnp.logical_not(mine))
-        def _():
-            for copy in to_owner(p, 0):
-                copy.start()
-
-        for dy in (1, 3, 2):
-            for copy in to_owner(p, dy):
-                copy.start()
+                half_state = jnp.concatenate(blocks[i][2 * c : 2 * c + 2], axis=0).astype(BF16)
+                for k in range(SIDE):
+                    st[p, c, k] = half_state[:, k * 256 : k * 256 + 256]
+            mine = pair_of(p) == z
+
+            @pl.when(mine)
+            def _(p=p):
+                rb[me] = st[p, core, y]
+                rbl[me] = stl[p, core]
+
+            @pl.when(jnp.logical_not(mine))
+            def _(p=p):
+                for copy in to_owner(p, 0, 0):
+                    copy.start()
+
+            for dy, dc in owners:
+                for copy in to_owner(p, dy, dc):
+                    copy.start()
 
     get_ku.wait()
     get_nl.wait()
@@ -371,16 +324,13 @@
 
     project(range(SIDE - 1))
     work(SIDE - 1, 0, False)
-    for p in range(SIDE - 1):
-        join(p)
     work(SIDE - 1, 1, False)
     project([SIDE - 1])
-    join(SIDE - 1)
-
-    def from_owner(source):
+
+    def from_peer(source):
         return (
             pltpu.make_async_remote_copy(
-                src_ref=cb.at[0, 0],
+                src_ref=st.at[0, 0, 0],
                 dst_ref=rb.at[source],
                 send_sem=r_send.at[0],
                 recv_sem=r_recv.at[source],
@@ -388,26 +338,28 @@
                 device_id_type=MESH,
             ),
             pltpu.make_async_remote_copy(
-                src_ref=cbl.at[0],
+                src_ref=stl.at[0, 0],
                 dst_ref=rbl.at[source],
                 send_sem=r_send.at[0],
-                recv_sem=r_recv.at[16 + source],
+                recv_sem=r_recv.at[rows + source],
                 device_id={"ctx": sibling},
                 device_id_type=MESH,
             ),
         )
 
-    for dy, dz in others:
-        for copy in from_owner(at(dy, dz) // 2):
+    for d in everyone:
+        for copy in from_peer(at(*d)):
             copy.wait_recv()
 
-    logs = rbl[...]
-    top = jnp.max(logs, axis=0)
-    w = jnp.exp2(logs - top[None])
-    w = w / jnp.sum(w, axis=0)[None]
+    stats = rbl[...]
+    top = jnp.max(stats, axis=0)
+    w = jnp.exp2(stats - top[None])
+    totals = pltpu.roll(stats.reshape(rows * 8, LANES), LANES - 16, 1).reshape(rows, 8, LANES)
+    w = w / jnp.sum(w * totals, axis=0)[None]
+    w = pltpu.roll(w.reshape(rows * 8, LANES), lax.rem(LANES - 2 * y, LANES), 1)
     acc = jnp.zeros((16, 256), F32)
-    for s in range(SIDE * SIDE):
-        f = pltpu.roll(w[s], lax.rem(LANES - 2 * y, LANES), 1)
+    for s in range(rows):
+        f = w[s * 8 : s * 8 + 8]
         f = [jnp.broadcast_to(f[:, i : i + 1], (8, LANES)) for i in (0, 1, 8, 9)]
         f = jnp.concatenate(
             [jnp.concatenate(f[:2], axis=1), jnp.concatenate(f[2:], axis=1)], axis=0
@@ -419,33 +371,19 @@
     def send_h(to, source):
         return pltpu.make_async_remote_copy(
             src_ref=ho,
-            dst_ref=hg.at[core, lax.rem(source, SIDE), source // SIDE],
-            send_sem=h_send.at[to // 2],
+            dst_ref=hg.at[
+                lax.rem(source, 2), lax.rem(source // 2, SIDE), source // (2 * SIDE)
+            ],
+            send_sem=h_send.at[to],
             recv_sem=h_recv.at[source],
             device_id={"ctx": to},
             device_id_type=MESH,
         )
 
-    def forward(of_core, dz):
-        slot = lax.rem(z + dz, SIDE)
-        return pltpu.make_async_remote_copy(
-            src_ref=hg.at[of_core, slot],
-            dst_ref=hg.at[of_core, slot],
-            send_sem=f_send.at[dz],
-            recv_sem=f_recv.at[slot],
-            device_id={"ctx": sibling},
-            device_id_type=MESH,
-        )
-
-    for dy, dz in others:
-        send_h(at(dy, dz), me // 2).start()
-    for dz in (0, 1, 3, 2):
-        for dy in range(SIDE):
-            if dy or dz:
-                send_h(at(dy, dz), at(dy, dz) // 2).wait_recv()
-        forward(core, dz).start()
-    for dz in range(SIDE):
-        forward(1 - core, dz).wait_recv()
+    for d in everyone:
+        send_h(at(*d), me).start()
+    for d in everyone:
+        send_h(at(*d), at(*d)).wait_recv()
 
     total = jnp.zeros((rows, out.shape[1]), F32)
     for c in range(2):
@@ -482,21 +420,17 @@
     for copy in q_sends:
         copy.wait_send()
     for p in range(SIDE):
-        for copy in to_sibling(p):
-            copy.wait_send()
 
         @pl.when(pair_of(p) != z)
         def _(p=p):
-            for copy in to_owner(p, 0):
+            for copy in to_owner(p, 0, 0):
                 copy.wait_send()
 
-        for dy in range(1, SIDE):
-            for copy in to_owner(p, dy):
+        for dy, dc in owners:
+            for copy in to_owner(p, dy, dc):
                 copy.wait_send()
-    for dy, dz in others:
-        send_h(at(dy, dz), me // 2).wait_send()
-    for dz in range(SIDE):
-        forward(core, dz).wait_send()
+    for d in everyone:
+        send_h(at(*d), me).wait_send()
     for i in range(1, groups):
         send_x(lax.rem(group + i, groups), group).wait_send()
 
@@ -510,7 +444,6 @@
     vdim = value_up.shape[2]
     columns = out_proj.shape[0]
     per = rows // reqs * heads
-    chips = SIDE * SIDE
     hbm = pl.BlockSpec(memory_space=pl.ANY)
     dma = pltpu.SemaphoreType.DMA
     return pl.pallas_call(
@@ -533,14 +466,10 @@
             pltpu.VMEM((SIDE, 2 * per, latent), BF16),
             pltpu.VMEM((SIDE, 8, LANES), F32),
             pltpu.VMEM((SIDE, 8, LANES), F32),
-            pltpu.VMEM((SIDE, 2, 16, 1024), BF16),
+            pltpu.VMEM((SIDE, 2, SIDE, 16, 256), BF16),
             pltpu.VMEM((SIDE, 2, 8, LANES), F32),
-            pltpu.VMEM((SIDE, 16, 1024), BF16),
-            pltpu.VMEM((SIDE, 8, LANES), F32),
-            pltpu.VMEM((SIDE, SIDE, 16, 256), BF16),
-            pltpu.VMEM((SIDE, 8, LANES), F32),
-            pltpu.VMEM((chips, 16, 256), BF16),
-            pltpu.VMEM((chips, 8, LANES), F32),
+            pltpu.VMEM((rows, 16, 256), BF16),
+            pltpu.VMEM((rows, 8, LANES), F32),
             pltpu.VMEM((16, 256), BF16),
             pltpu.VMEM((2, SIDE, SIDE, 16, 256), BF16),
             pltpu.VMEM((groups, rows, columns), BF16),
@@ -548,14 +477,10 @@
             dma((6,)),
             dma((31,)),
             dma((rows,)),
-            dma((2 * SIDE,)),
-            dma((2 * SIDE,)),
-            dma((2 * chips,)),
-            dma((2 * chips,)),
-            dma((chips,)),
-            dma((chips,)),
-            dma((SIDE,)),
-            dma((SIDE,)),
+            dma((2 * rows,)),
+            dma((2 * rows,)),
+            dma((rows,)),
+            dma((rows,)),
             dma((groups,)),
             dma((groups,)),
         ],

time: 47 us -> 45.9 us (0.977)
  Pallas kernels: 45.4 us -> 44.3 us
    pallas_call x1, Pallas kernels: 45.4 us -> 44.3 us  [local(): pl.pallas_call(functools.partial(kernel, groups), out_shape=jax.ShapeDtyp...]
where the time goes in v6:
time: 45.9 us; the launch traced here: 45.6 us
  Pallas kernels  44.3 us (97%)
  local copies, waits for them, and re-layouts  1.32 us (3%)
    pallas_call x1, Pallas kernels, local(): pl.pallas_call(functools.partial(kernel, groups), out_shape=jax.ShapeDtyp...  44.3 us
    unnamed x1, local copies, waits for them, and re-layouts  1.32 us

profile of v6, /device:TPU:1, one launch (start us, length us, event | category | flops | bytes accessed | tf_op | source)
XLA Modules:
  0.0 45.6 jit_solution(4216959760252872201)
XLA Ops:
  0.0 44.3 %mla_decode.1 = bf16[32,224]{1,0:T(8,128)(2,1)} custom-call(bf16[1,32,192]{2,1,0:T(8,128)(2,1)} %queries.1, bf16[8,576,1536]{2,1,0:T(8,128)(2,1)} %bitcast.2, bf16[32,576]{1,0:T(8,128)(2,1)} %fresh.1, s32[8]{0:T(128)} %lengths_in.1, bf16[32,128,512]{2,1,0:T(8,128)(2,1)} %key_up.1, bf16[32,512,128]{2,1,0:T(8,128)(2,1)} %value_up.1, bf16[224,4096]{1,0:T(8,128)(2,1)} %bitcast.3), custom_call_target="tpu_custom_call" | custom-call | flops 4000000000 | bytes 25000000 | tf_op jit(solution)/shard_map/mla_decode/pallas_call | solution.py:449
  44.3 1.3 %copy.9 = bf16[32,224]{1,0:T(8,128)(2,1)} copy(bf16[32,224]{1,0:T(8,128)(2,1)} %mla_decode.1) | data formatting | bytes 28672

commit v7 on v6

--- a/solution.py
+++ b/solution.py
@@ -31,6 +31,7 @@
     ku,
     vu,
     op,
+    opt,
     nl,
     lengths,
     qown,
@@ -347,6 +348,13 @@
             ),
         )
 
+    @pl.loop(0, heads * LANES // 512)
+    def _(i):
+        span = pl.ds(pl.multiple_of(i * 512, 512), 512)
+        opt[span, :] = jnp.transpose(op[:, span])
+
+    for copy in q_sends:
+        copy.wait_send()
     for d in everyone:
         for copy in from_peer(at(*d)):
             copy.wait_recv()
@@ -382,6 +390,16 @@
 
     for d in everyone:
         send_h(at(*d), me).start()
+    for p in range(SIDE):
+
+        @pl.when(pair_of(p) != z)
+        def _(p=p):
+            for copy in to_owner(p, 0, 0):
+                copy.wait_send()
+
+        for dy, dc in owners:
+            for copy in to_owner(p, dy, dc):
+                copy.wait_send()
     for d in everyone:
         send_h(at(*d), at(*d)).wait_recv()
 
@@ -392,8 +410,8 @@
             for u in range(2):
                 lhs = jnp.concatenate([a[u * 8 : u * 8 + 8] for a in x], axis=0).astype(BF16)
                 first = (c * 16 + u * 8 + i * 2) * LANES
-                total = total + lax.dot_general(
-                    lhs, op[:, first : first + 256], contract, preferred_element_type=F32
+                total = total + jnp.dot(
+                    lhs, opt[first : first + 256, :], preferred_element_type=F32
                 )
     xb[group] = total.astype(BF16)
 
@@ -409,6 +427,8 @@
 
     for i in range(1, groups):
         send_x(lax.rem(group + i, groups), group).start()
+    for d in everyone:
+        send_h(at(*d), me).wait_send()
     for i in range(1, groups):
         other = lax.rem(group + i, groups)
         send_x(other, other).wait_recv()
@@ -417,20 +437,6 @@
         result = result + xb[g].astype(F32)
     out[...] = result.astype(out.dtype)
 
-    for copy in q_sends:
-        copy.wait_send()
-    for p in range(SIDE):
-
-        @pl.when(pair_of(p) != z)
-        def _(p=p):
-            for copy in to_owner(p, 0, 0):
-                copy.wait_send()
-
-        for dy, dc in owners:
-            for copy in to_owner(p, dy, dc):
-                copy.wait_send()
-    for d in everyone:
-        send_h(at(*d), me).wait_send()
     for i in range(1, groups):
         send_x(lax.rem(group + i, groups), group).wait_send()
 
@@ -457,6 +463,7 @@
             pltpu.VMEM((heads, nope, latent), BF16),
             pltpu.VMEM((heads, latent, vdim), BF16),
             pltpu.VMEM((columns, heads * vdim), BF16),
+            pltpu.VMEM((heads * vdim, columns), BF16),
             pltpu.VMEM((rows, width), BF16),
             pltpu.SMEM((reqs,), jnp.int32),
             pltpu.VMEM((heads, queries.shape[2]), BF16),

time: 45.9 us -> 45.4 us (0.989)
  Pallas kernels: 44.3 us -> 43.8 us
    pallas_call x1, Pallas kernels: 44.3 us -> 43.8 us  [local(): pl.pallas_call(functools.partial(kernel, groups), out_shape=jax.ShapeDtyp...]
where the time goes in v7:
time: 45.4 us; the launch traced here: 45.1 us
  Pallas kernels  43.8 us (96%)
  local copies, waits for them, and re-layouts  1.32 us (3%)
    pallas_call x1, Pallas kernels, local(): pl.pallas_call(functools.partial(kernel, groups), out_shape=jax.ShapeDtyp...  43.8 us
    unnamed x1, local copies, waits for them, and re-layouts  1.32 us

profile of v7, /device:TPU:1, one launch (start us, length us, event | category | flops | bytes accessed | tf_op | source)
XLA Modules:
  0.0 45.1 jit_solution(17470274803393025882)
XLA Ops:
  0.0 43.8 %mla_decode.1 = bf16[32,224]{1,0:T(8,128)(2,1)} custom-call(bf16[1,32,192]{2,1,0:T(8,128)(2,1)} %queries.1, bf16[8,576,1536]{2,1,0:T(8,128)(2,1)} %bitcast.2, bf16[32,576]{1,0:T(8,128)(2,1)} %fresh.1, s32[8]{0:T(128)} %lengths_in.1, bf16[32,128,512]{2,1,0:T(8,128)(2,1)} %key_up.1, bf16[32,512,128]{2,1,0:T(8,128)(2,1)} %value_up.1, bf16[224,4096]{1,0:T(8,128)(2,1)} %bitcast.3), custom_call_target="tpu_custom_call" | custom-call | flops 4000000000 | bytes 25000000 | tf_op jit(solution)/shard_map/mla_decode/pallas_call | solution.py:455
  43.8 1.3 %copy.9 = bf16[32,224]{1,0:T(8,128)(2,1)} copy(bf16[32,224]{1,0:T(8,128)(2,1)} %mla_decode.1) | data formatting | bytes 28672

commit v8 on v7

--- a/solution.py
+++ b/solution.py
@@ -313,11 +313,11 @@
         got_q(at(dy, dz))
         q_sends[19 + i].start()
     work(0, 0, True)
+    work(0, 1, True)
     for dy in range(1, SIDE):
         for dz in range(SIDE):
             got_q(at(dy, dz, 1))
     absorb([pair_of(p) for p in range(1, SIDE)])
-    work(0, 1, True)
     @pl.loop(1, SIDE - 1)
     def _(p):
         work(p, 0, False)
@@ -403,16 +403,14 @@
     for d in everyone:
         send_h(at(*d), at(*d)).wait_recv()
 
-    total = jnp.zeros((rows, out.shape[1]), F32)
+    parts = []
     for c in range(2):
-        for i in range(SIDE):
-            x = [hg[c, pair, i].astype(F32) for pair in range(SIDE)]
-            for u in range(2):
-                lhs = jnp.concatenate([a[u * 8 : u * 8 + 8] for a in x], axis=0).astype(BF16)
-                first = (c * 16 + u * 8 + i * 2) * LANES
-                total = total + jnp.dot(
-                    lhs, opt[first : first + 256, :], preferred_element_type=F32
-                )
+        x = [[hg[c, pair, i].astype(F32) for pair in range(SIDE)] for i in range(SIDE)]
+        for u in range(2):
+            for i in range(SIDE):
+                part = jnp.concatenate([a[u * 8 : u * 8 + 8] for a in x[i]], axis=0)
+                parts.append(part.astype(BF16))
+    total = jnp.dot(jnp.concatenate(parts, axis=1), opt[...], preferred_element_type=F32)
     xb[group] = total.astype(BF16)
 
     def send_x(to, slot):

time: 45.4 us -> 44.7 us (0.985)
  Pallas kernels: 43.8 us -> 43.2 us
    pallas_call x1, Pallas kernels: 43.8 us -> 43.2 us  [local(): pl.pallas_call(functools.partial(kernel, groups), out_shape=jax.ShapeDtyp...]
where the time goes in v8:
time: 44.7 us; the launch traced here: 44.5 us
  Pallas kernels  43.2 us (97%)
  local copies, waits for them, and re-layouts  1.32 us (3%)
    pallas_call x1, Pallas kernels, local(): pl.pallas_call(functools.partial(kernel, groups), out_shape=jax.ShapeDtyp...  43.2 us
    unnamed x1, local copies, waits for them, and re-layouts  1.32 us

profile of v8, /device:TPU:1, one launch (start us, length us, event | category | flops | bytes accessed | tf_op | source)
XLA Modules:
  0.0 44.5 jit_solution(2128849527461933441)
XLA Ops:
  0.0 43.2 %mla_decode.1 = bf16[32,224]{1,0:T(8,128)(2,1)} custom-call(bf16[1,32,192]{2,1,0:T(8,128)(2,1)} %queries.1, bf16[8,576,1536]{2,1,0:T(8,128)(2,1)} %bitcast.2, bf16[32,576]{1,0:T(8,128)(2,1)} %fresh.1, s32[8]{0:T(128)} %lengths_in.1, bf16[32,128,512]{2,1,0:T(8,128)(2,1)} %key_up.1, bf16[32,512,128]{2,1,0:T(8,128)(2,1)} %value_up.1, bf16[224,4096]{1,0:T(8,128)(2,1)} %bitcast.3), custom_call_target="tpu_custom_call" | custom-call | flops 4000000000 | bytes 25000000 | tf_op jit(solution)/shard_map/mla_decode/pallas_call | solution.py:453
  43.2 1.3 %copy.9 = bf16[32,224]{1,0:T(8,128)(2,1)} copy(bf16[32,224]{1,0:T(8,128)(2,1)} %mla_decode.1) | data formatting | bytes 28672
